TPU v7x, 256 devices: a whole 4x4x8 slice. The times are simulated.
256 devices in a mesh: ens: 16 (over z, y_hi), space: 16 (over x, y_lo, core).
Axes of the slice: x: 4, y: 4 (y_hi: 2, y_lo: 2; y = y_hi * 2 + y_lo), z: 8, core: 2. Of those that a mesh axis runs over, the one named last changes fastest.
Arguments:
- hidden_vectors: bfloat16 [16, 192, 720, 128], P('ens', 'space'), may hold values from -6 to 6
- target: float32 [2, 192, 720], P(None, 'space', 'ens'), may hold values from -6 to 6
- mix_weight: bfloat16 [2, 9, 128, 128], replicated, may hold values from -0.5 to 0.5
- basis_coef: bfloat16 [2, 9, 4, 3, 192], replicated, may hold values from -0.796875 to 0.796875
- rescaling_factors: float32 [2, 2, 128], replicated, may hold values from 0.1 to 1.9
- up_weight: bfloat16 [2, 128, 256], replicated, may hold values from -0.5 to 0.5
- down_weight: bfloat16 [2, 256, 128], replicated, may hold values from -0.375 to 0.375
- readout_matrix: bfloat16 [2, 128], replicated, may hold values from -0.5 to 0.5
- band_start: int32 [192], replicated, may hold values from -2 to 193, as said below
- band_width: int32 [192], replicated, may hold values from 1 to 4, as said below
Outputs:
- predicted_latents: bfloat16 [16, 192, 720, 128], P('ens', 'space')
- probabilistic_score: float32 [2, 192, 720], P(None, 'space', 'ens')
Inputs may be any that keep to these rules, and one draw needn't show every extreme that they name: Every output latitude o has a band of band_width[o] rows; the first latitude's band has 4 rows and the last latitude's band one row. band_start[o] lies between o - 2 and o + 3 - band_width[o]; the first latitude's band starts at -2 and the last latitude's band ends at 193.
All inputs are finite; a program needn't handle non-finite values.
Results may differ from a plain program's by a relative error of at most 0.015.
Values may be sent and summed in bfloat16 or wider, within the bound.
A program may use at most 64 MiB of HBM per device.

v0:
```python
import jax
import jax.numpy as jnp
from jax import lax
from jax.sharding import PartitionSpec as P

K = 9
BMAX = 4
HALO = 2
LW = 3
BLOCKS = 2


def extended(array, sides, width):
    for axis, dim in sides:
        peers, length = (lax.axis_size(axis), array.shape[dim])
        up = [(i, (i + 1) % peers) for i in range(peers - 1)]
        down = [(j, i) for i, j in up]
        last = lax.slice_in_dim(array, length - width, length, axis=dim)
        initial = lax.slice_in_dim(array, 0, width, axis=dim)
        before = lax.ppermute(last, axis, up)
        after = lax.ppermute(initial, axis, down)
        array = jnp.concatenate([before, array, after], axis=dim)
    return array


def normalize(values, row_gain):
    widened = values.astype(jnp.float32)
    inv_scale = lax.rsqrt(jnp.mean(widened * widened, axis=-1, keepdims=True) + 1e-06)
    return (widened * inv_scale * row_gain).astype(jnp.bfloat16)


def wrap_longitude(grid_field):
    radius = LW // 2
    return jnp.concatenate([grid_field[:, -radius:], grid_field, grid_field[:, :radius]], axis=1)


def band_matrix(coef, rel_start, widths):
    offsets = jnp.arange(BMAX, dtype=jnp.int32)
    window = jnp.arange(2 * HALO + 1, dtype=jnp.int32)
    inside = offsets[:, None, None] < widths[None, :, None]
    placed_field = window[None, None, :] == rel_start[None, :, None] + offsets[:, None, None]
    select = jnp.where(inside & placed_field, 1.0, 0.0).astype(jnp.float32)
    return jnp.einsum("kqlo,qor->klor", coef.astype(jnp.float32), select).astype(jnp.bfloat16)


def disco_rows(padded, bands, mixing_weight):
    row_count = bands.shape[2]
    lon_count = padded.shape[1] - (LW - 1)
    channels = padded.shape[2]
    window_rows = 2 * HALO + 1

    def one_row(row):
        window = lax.dynamic_slice_in_dim(padded, row, window_rows, 0)
        row_weights = lax.dynamic_index_in_dim(bands, row, 2, keepdims=False).astype(jnp.float32)
        total = jnp.zeros((K, lon_count, channels), jnp.float32)
        for lat_offset in range(window_rows):
            for shift in range(LW):
                source = window[lat_offset, shift : shift + lon_count].astype(jnp.float32)
                total = total + row_weights[:, shift, lat_offset][:, None, None] * source[None]
        gathered = total.astype(jnp.bfloat16)
        return jnp.einsum(
            "kjc,kcd->jd", gathered, mixing_weight, preferred_element_type=jnp.float32
        )

    return lax.map(one_row, jnp.arange(row_count, dtype=jnp.int32))


def block_tail(present_state, conv_sum, row_gain, up_matrix, down_matrix):
    carried_state = (present_state.astype(jnp.float32) + conv_sum).astype(jnp.bfloat16)
    normed = normalize(carried_state, row_gain)
    channels = normed.shape[-1]
    hidden = jax.nn.gelu(
        jnp.dot(normed.reshape(-1, channels), up_matrix, preferred_element_type=jnp.float32),
        approximate=False,
    ).astype(jnp.bfloat16)
    output = jnp.dot(hidden, down_matrix, preferred_element_type=jnp.float32).reshape(
        carried_state.shape
    )
    return (carried_state.astype(jnp.float32) + output).astype(jnp.bfloat16)


def body(
    hidden_vectors,
    target,
    mix_weight,
    basis_coef,
    rescaling_factors,
    up_weight,
    down_weight,
    readout_matrix,
    band_start,
    band_width,
):
    lat_rows = hidden_vectors.shape[1]
    row_first = lax.axis_index("space") * lat_rows
    global_rows = row_first + jnp.arange(lat_rows, dtype=jnp.int32)
    local_start = lax.dynamic_slice_in_dim(band_start, row_first, lat_rows)
    local_width = lax.dynamic_slice_in_dim(band_width, row_first, lat_rows)
    rel_start = local_start - global_rows + HALO
    present_state = hidden_vectors
    for block_index in range(BLOCKS):
        normed = normalize(present_state, rescaling_factors[block_index, 0])
        padded = extended(normed, (("space", 1),), HALO)
        wrapped = wrap_longitude(padded[0])
        row_coef = lax.dynamic_slice_in_dim(basis_coef[block_index], row_first, lat_rows, axis=3)
        bands = band_matrix(row_coef, rel_start, local_width)
        conv_sum = disco_rows(wrapped, bands, mix_weight[block_index])
        present_state = block_tail(
            present_state,
            conv_sum[None],
            rescaling_factors[block_index, 1],
            up_weight[block_index],
            down_weight[block_index],
        )
    lowest_level_prediction = jnp.einsum(
        "uzgm,wm->uwzg", present_state, readout_matrix, preferred_element_type=jnp.float32
    )
    lon_cols = target.shape[2]
    all_members = lax.all_gather(
        lowest_level_prediction.astype(jnp.bfloat16), "ens", axis=0, tiled=True
    ).astype(lowest_level_prediction.dtype)
    members = lax.dynamic_slice_in_dim(
        all_members, lax.axis_index("ens") * lon_cols, lon_cols, axis=3
    )
    member_count = members.shape[0]
    skill_term = jnp.mean(jnp.abs(members - target[None]), axis=0)
    spread_sum = jnp.sum(jnp.abs(members[:, None] - members[None]), axis=(0, 1))
    probabilistic_score = skill_term - spread_sum / (2.0 * member_count * (member_count - 1))
    return (present_state, probabilistic_score)


def solution(mesh):
    in_specs = (
        P("ens", "space", None, None),
        P(None, "space", "ens"),
        P(),
        P(),
        P(),
        P(),
        P(),
        P(),
        P(),
        P(),
    )
    out_specs = (P("ens", "space", None, None), P(None, "space", "ens"))
    return jax.shard_map(body, mesh=mesh, in_specs=in_specs, out_specs=out_specs, check_vma=False)
```

profile of v0, /device:TPU:1, one launch (start us, length us, event | category | flops | bytes accessed | tf_op | source)
XLA Modules:
  0.0 477.9 jit_solution(11918143593230030859)
XLA Ops:
  9.0 4.6 collective-permute-start
  27.4 162.8 %while.20 = (s32[]{:T(128)}, f32[12,720,128]{2,1,0:T(8,128)}, s32[12]{0:T(128)S(1)}, bf16[9,3,12,5]{0,3,1,2:T(8,128)(2,1)}, bf16[16,722,128]{2,1,0:T(8,128)(2,1)...) while((s32[]{:T(128)}, f32[12,720,128]{2,1,0:T(8,128)}, ...), condition=%wide.region_2.3_spmd, body=%wide.region_1.2_spmd.sunk | while | flops 238602384 | bytes 14490802 | solution.py:65
  33.9 7.1 %fusion.139 = f32[12,720,128]{2,1,0:T(8,128)} fusion(f32[12,720,128]{2,1,0:T(8,128)} %get-tuple-element.389, s32[]{:T(128)} %get-tuple-element.388, bf16[9,128,128]{2,1,0:T(8,128)(2,1)} %get-tuple-element.407, f32[720,128]{1,0:T(8,128)} %get-tuple-element.308, f32[9]{0:T(128)S(1)} %get-tuple-element.309, f32[720,128]{1,0:T(8,128)} %get-tuple-element.310, ...), kind=kOutput, calls=%fused_computation.3.clone.1 | convolution fusion | flops 237219840 | bytes 6194204 | tf_op jit(solution)/shard_map/while/body/eval_jaxpr/kjc,kcd->jd/dot_general | solution.py:61
  47.5 7.1 %fusion.139 = f32[12,720,128]{2,1,0:T(8,128)} fusion(f32[12,720,128]{2,1,0:T(8,128)} %get-tuple-element.389, s32[]{:T(128)} %get-tuple-element.388, bf16[9,128,128]{2,1,0:T(8,128)(2,1)} %get-tuple-element.407, f32[720,128]{1,0:T(8,128)} %get-tuple-element.308, f32[9]{0:T(128)S(1)} %get-tuple-element.309, f32[720,128]{1,0:T(8,128)} %get-tuple-element.310, ...), kind=kOutput, calls=%fused_computation.3.clone.1 | convolution fusion | flops 237219840 | bytes 6194204 | tf_op jit(solution)/shard_map/while/body/eval_jaxpr/kjc,kcd->jd/dot_general | solution.py:61
  61.0 7.1 %fusion.139 = f32[12,720,128]{2,1,0:T(8,128)} fusion(f32[12,720,128]{2,1,0:T(8,128)} %get-tuple-element.389, s32[]{:T(128)} %get-tuple-element.388, bf16[9,128,128]{2,1,0:T(8,128)(2,1)} %get-tuple-element.407, f32[720,128]{1,0:T(8,128)} %get-tuple-element.308, f32[9]{0:T(128)S(1)} %get-tuple-element.309, f32[720,128]{1,0:T(8,128)} %get-tuple-element.310, ...), kind=kOutput, calls=%fused_computation.3.clone.1 | convolution fusion | flops 237219840 | bytes 6194204 | tf_op jit(solution)/shard_map/while/body/eval_jaxpr/kjc,kcd->jd/dot_general | solution.py:61
  74.6 7.1 %fusion.139 = f32[12,720,128]{2,1,0:T(8,128)} fusion(f32[12,720,128]{2,1,0:T(8,128)} %get-tuple-element.389, s32[]{:T(128)} %get-tuple-element.388, bf16[9,128,128]{2,1,0:T(8,128)(2,1)} %get-tuple-element.407, f32[720,128]{1,0:T(8,128)} %get-tuple-element.308, f32[9]{0:T(128)S(1)} %get-tuple-element.309, f32[720,128]{1,0:T(8,128)} %get-tuple-element.310, ...), kind=kOutput, calls=%fused_computation.3.clone.1 | convolution fusion | flops 237219840 | bytes 6194204 | tf_op jit(solution)/shard_map/while/body/eval_jaxpr/kjc,kcd->jd/dot_general | solution.py:61
  88.2 7.1 %fusion.139 = f32[12,720,128]{2,1,0:T(8,128)} fusion(f32[12,720,128]{2,1,0:T(8,128)} %get-tuple-element.389, s32[]{:T(128)} %get-tuple-element.388, bf16[9,128,128]{2,1,0:T(8,128)(2,1)} %get-tuple-element.407, f32[720,128]{1,0:T(8,128)} %get-tuple-element.308, f32[9]{0:T(128)S(1)} %get-tuple-element.309, f32[720,128]{1,0:T(8,128)} %get-tuple-element.310, ...), kind=kOutput, calls=%fused_computation.3.clone.1 | convolution fusion | flops 237219840 | bytes 6194204 | tf_op jit(solution)/shard_map/while/body/eval_jaxpr/kjc,kcd->jd/dot_general | solution.py:61
  101.7 7.1 %fusion.139 = f32[12,720,128]{2,1,0:T(8,128)} fusion(f32[12,720,128]{2,1,0:T(8,128)} %get-tuple-element.389, s32[]{:T(128)} %get-tuple-element.388, bf16[9,128,128]{2,1,0:T(8,128)(2,1)} %get-tuple-element.407, f32[720,128]{1,0:T(8,128)} %get-tuple-element.308, f32[9]{0:T(128)S(1)} %get-tuple-element.309, f32[720,128]{1,0:T(8,128)} %get-tuple-element.310, ...), kind=kOutput, calls=%fused_computation.3.clone.1 | convolution fusion | flops 237219840 | bytes 6194204 | tf_op jit(solution)/shard_map/while/body/eval_jaxpr/kjc,kcd->jd/dot_general | solution.py:61
  115.3 7.1 %fusion.139 = f32[12,720,128]{2,1,0:T(8,128)} fusion(f32[12,720,128]{2,1,0:T(8,128)} %get-tuple-element.389, s32[]{:T(128)} %get-tuple-element.388, bf16[9,128,128]{2,1,0:T(8,128)(2,1)} %get-tuple-element.407, f32[720,128]{1,0:T(8,128)} %get-tuple-element.308, f32[9]{0:T(128)S(1)} %get-tuple-element.309, f32[720,128]{1,0:T(8,128)} %get-tuple-element.310, ...), kind=kOutput, calls=%fused_computation.3.clone.1 | convolution fusion | flops 237219840 | bytes 6194204 | tf_op jit(solution)/shard_map/while/body/eval_jaxpr/kjc,kcd->jd/dot_general | solution.py:61
  128.9 7.1 %fusion.139 = f32[12,720,128]{2,1,0:T(8,128)} fusion(f32[12,720,128]{2,1,0:T(8,128)} %get-tuple-element.389, s32[]{:T(128)} %get-tuple-element.388, bf16[9,128,128]{2,1,0:T(8,128)(2,1)} %get-tuple-element.407, f32[720,128]{1,0:T(8,128)} %get-tuple-element.308, f32[9]{0:T(128)S(1)} %get-tuple-element.309, f32[720,128]{1,0:T(8,128)} %get-tuple-element.310, ...), kind=kOutput, calls=%fused_computation.3.clone.1 | convolution fusion | flops 237219840 | bytes 6194204 | tf_op jit(solution)/shard_map/while/body/eval_jaxpr/kjc,kcd->jd/dot_general | solution.py:61
  142.5 7.1 %fusion.139 = f32[12,720,128]{2,1,0:T(8,128)} fusion(f32[12,720,128]{2,1,0:T(8,128)} %get-tuple-element.389, s32[]{:T(128)} %get-tuple-element.388, bf16[9,128,128]{2,1,0:T(8,128)(2,1)} %get-tuple-element.407, f32[720,128]{1,0:T(8,128)} %get-tuple-element.308, f32[9]{0:T(128)S(1)} %get-tuple-element.309, f32[720,128]{1,0:T(8,128)} %get-tuple-element.310, ...), kind=kOutput, calls=%fused_computation.3.clone.1 | convolution fusion | flops 237219840 | bytes 6194204 | tf_op jit(solution)/shard_map/while/body/eval_jaxpr/kjc,kcd->jd/dot_general | solution.py:61
  156.0 7.1 %fusion.139 = f32[12,720,128]{2,1,0:T(8,128)} fusion(f32[12,720,128]{2,1,0:T(8,128)} %get-tuple-element.389, s32[]{:T(128)} %get-tuple-element.388, bf16[9,128,128]{2,1,0:T(8,128)(2,1)} %get-tuple-element.407, f32[720,128]{1,0:T(8,128)} %get-tuple-element.308, f32[9]{0:T(128)S(1)} %get-tuple-element.309, f32[720,128]{1,0:T(8,128)} %get-tuple-element.310, ...), kind=kOutput, calls=%fused_computation.3.clone.1 | convolution fusion | flops 237219840 | bytes 6194204 | tf_op jit(solution)/shard_map/while/body/eval_jaxpr/kjc,kcd->jd/dot_general | solution.py:61
  169.6 7.1 %fusion.139 = f32[12,720,128]{2,1,0:T(8,128)} fusion(f32[12,720,128]{2,1,0:T(8,128)} %get-tuple-element.389, s32[]{:T(128)} %get-tuple-element.388, bf16[9,128,128]{2,1,0:T(8,128)(2,1)} %get-tuple-element.407, f32[720,128]{1,0:T(8,128)} %get-tuple-element.308, f32[9]{0:T(128)S(1)} %get-tuple-element.309, f32[720,128]{1,0:T(8,128)} %get-tuple-element.310, ...), kind=kOutput, calls=%fused_computation.3.clone.1 | convolution fusion | flops 237219840 | bytes 6194204 | tf_op jit(solution)/shard_map/while/body/eval_jaxpr/kjc,kcd->jd/dot_general | solution.py:61
  183.1 7.1 %fusion.139 = f32[12,720,128]{2,1,0:T(8,128)} fusion(f32[12,720,128]{2,1,0:T(8,128)} %get-tuple-element.389, s32[]{:T(128)} %get-tuple-element.388, bf16[9,128,128]{2,1,0:T(8,128)(2,1)} %get-tuple-element.407, f32[720,128]{1,0:T(8,128)} %get-tuple-element.308, f32[9]{0:T(128)S(1)} %get-tuple-element.309, f32[720,128]{1,0:T(8,128)} %get-tuple-element.310, ...), kind=kOutput, calls=%fused_computation.3.clone.1 | convolution fusion | flops 237219840 | bytes 6194204 | tf_op jit(solution)/shard_map/while/body/eval_jaxpr/kjc,kcd->jd/dot_general | solution.py:61
  190.2 4.3 fusion.60
  196.0 20.5 %fusion.38 = bf16[8640,256]{1,0:T(8,128)(2,1)S(1)} fusion(bf16[8640,128]{1,0:T(8,128)(2,1)S(1)} %bitcast.340, bf16[2,128,256]{2,1,0:T(8,128)(2,1)S(1)} %copy-done.13), kind=kOutput, calls=%fused_computation.104 | convolution fusion | flops 710000640 | bytes 6701056 | tf_op jit(solution)/shard_map/dot_general | solution.py:73
  237.6 167.8 %while.21 = (s32[]{:T(128)}, f32[12,720,128]{2,1,0:T(8,128)}, s32[12]{0:T(128)S(1)}, bf16[9,3,12,5]{0,3,1,2:T(8,128)(2,1)}, bf16[16,722,128]{2,1,0:T(8,128)(2,1)...) while((s32[]{:T(128)}, f32[12,720,128]{2,1,0:T(8,128)}, ...), condition=%wide.region_6.7_spmd, body=%wide.region_5.6_spmd.sunk | while | flops 238602384 | bytes 14490802 | solution.py:65
  244.5 7.1 %fusion.142 = f32[12,720,128]{2,1,0:T(8,128)} fusion(f32[12,720,128]{2,1,0:T(8,128)} %get-tuple-element.431, s32[]{:T(128)} %get-tuple-element.430, bf16[9,128,128]{2,1,0:T(8,128)(2,1)} %get-tuple-element.449, f32[720,128]{1,0:T(8,128)} %get-tuple-element.344, f32[9]{0:T(128)S(1)} %get-tuple-element.345, f32[720,128]{1,0:T(8,128)} %get-tuple-element.346, ...), kind=kOutput, calls=%fused_computation.53.clone.1 | convolution fusion | flops 237219840 | bytes 6194204 | tf_op jit(solution)/shard_map/while/body/eval_jaxpr/kjc,kcd->jd/dot_general | solution.py:61
  258.5 7.1 %fusion.142 = f32[12,720,128]{2,1,0:T(8,128)} fusion(f32[12,720,128]{2,1,0:T(8,128)} %get-tuple-element.431, s32[]{:T(128)} %get-tuple-element.430, bf16[9,128,128]{2,1,0:T(8,128)(2,1)} %get-tuple-element.449, f32[720,128]{1,0:T(8,128)} %get-tuple-element.344, f32[9]{0:T(128)S(1)} %get-tuple-element.345, f32[720,128]{1,0:T(8,128)} %get-tuple-element.346, ...), kind=kOutput, calls=%fused_computation.53.clone.1 | convolution fusion | flops 237219840 | bytes 6194204 | tf_op jit(solution)/shard_map/while/body/eval_jaxpr/kjc,kcd->jd/dot_general | solution.py:61
  272.4 7.1 %fusion.142 = f32[12,720,128]{2,1,0:T(8,128)} fusion(f32[12,720,128]{2,1,0:T(8,128)} %get-tuple-element.431, s32[]{:T(128)} %get-tuple-element.430, bf16[9,128,128]{2,1,0:T(8,128)(2,1)} %get-tuple-element.449, f32[720,128]{1,0:T(8,128)} %get-tuple-element.344, f32[9]{0:T(128)S(1)} %get-tuple-element.345, f32[720,128]{1,0:T(8,128)} %get-tuple-element.346, ...), kind=kOutput, calls=%fused_computation.53.clone.1 | convolution fusion | flops 237219840 | bytes 6194204 | tf_op jit(solution)/shard_map/while/body/eval_jaxpr/kjc,kcd->jd/dot_general | solution.py:61
  286.4 7.1 %fusion.142 = f32[12,720,128]{2,1,0:T(8,128)} fusion(f32[12,720,128]{2,1,0:T(8,128)} %get-tuple-element.431, s32[]{:T(128)} %get-tuple-element.430, bf16[9,128,128]{2,1,0:T(8,128)(2,1)} %get-tuple-element.449, f32[720,128]{1,0:T(8,128)} %get-tuple-element.344, f32[9]{0:T(128)S(1)} %get-tuple-element.345, f32[720,128]{1,0:T(8,128)} %get-tuple-element.346, ...), kind=kOutput, calls=%fused_computation.53.clone.1 | convolution fusion | flops 237219840 | bytes 6194204 | tf_op jit(solution)/shard_map/while/body/eval_jaxpr/kjc,kcd->jd/dot_general | solution.py:61
  300.4 7.1 %fusion.142 = f32[12,720,128]{2,1,0:T(8,128)} fusion(f32[12,720,128]{2,1,0:T(8,128)} %get-tuple-element.431, s32[]{:T(128)} %get-tuple-element.430, bf16[9,128,128]{2,1,0:T(8,128)(2,1)} %get-tuple-element.449, f32[720,128]{1,0:T(8,128)} %get-tuple-element.344, f32[9]{0:T(128)S(1)} %get-tuple-element.345, f32[720,128]{1,0:T(8,128)} %get-tuple-element.346, ...), kind=kOutput, calls=%fused_computation.53.clone.1 | convolution fusion | flops 237219840 | bytes 6194204 | tf_op jit(solution)/shard_map/while/body/eval_jaxpr/kjc,kcd->jd/dot_general | solution.py:61
  314.4 7.1 %fusion.142 = f32[12,720,128]{2,1,0:T(8,128)} fusion(f32[12,720,128]{2,1,0:T(8,128)} %get-tuple-element.431, s32[]{:T(128)} %get-tuple-element.430, bf16[9,128,128]{2,1,0:T(8,128)(2,1)} %get-tuple-element.449, f32[720,128]{1,0:T(8,128)} %get-tuple-element.344, f32[9]{0:T(128)S(1)} %get-tuple-element.345, f32[720,128]{1,0:T(8,128)} %get-tuple-element.346, ...), kind=kOutput, calls=%fused_computation.53.clone.1 | convolution fusion | flops 237219840 | bytes 6194204 | tf_op jit(solution)/shard_map/while/body/eval_jaxpr/kjc,kcd->jd/dot_general | solution.py:61
  328.4 7.1 %fusion.142 = f32[12,720,128]{2,1,0:T(8,128)} fusion(f32[12,720,128]{2,1,0:T(8,128)} %get-tuple-element.431, s32[]{:T(128)} %get-tuple-element.430, bf16[9,128,128]{2,1,0:T(8,128)(2,1)} %get-tuple-element.449, f32[720,128]{1,0:T(8,128)} %get-tuple-element.344, f32[9]{0:T(128)S(1)} %get-tuple-element.345, f32[720,128]{1,0:T(8,128)} %get-tuple-element.346, ...), kind=kOutput, calls=%fused_computation.53.clone.1 | convolution fusion | flops 237219840 | bytes 6194204 | tf_op jit(solution)/shard_map/while/body/eval_jaxpr/kjc,kcd->jd/dot_general | solution.py:61
  342.3 7.1 %fusion.142 = f32[12,720,128]{2,1,0:T(8,128)} fusion(f32[12,720,128]{2,1,0:T(8,128)} %get-tuple-element.431, s32[]{:T(128)} %get-tuple-element.430, bf16[9,128,128]{2,1,0:T(8,128)(2,1)} %get-tuple-element.449, f32[720,128]{1,0:T(8,128)} %get-tuple-element.344, f32[9]{0:T(128)S(1)} %get-tuple-element.345, f32[720,128]{1,0:T(8,128)} %get-tuple-element.346, ...), kind=kOutput, calls=%fused_computation.53.clone.1 | convolution fusion | flops 237219840 | bytes 6194204 | tf_op jit(solution)/shard_map/while/body/eval_jaxpr/kjc,kcd->jd/dot_general | solution.py:61
  356.3 7.1 %fusion.142 = f32[12,720,128]{2,1,0:T(8,128)} fusion(f32[12,720,128]{2,1,0:T(8,128)} %get-tuple-element.431, s32[]{:T(128)} %get-tuple-element.430, bf16[9,128,128]{2,1,0:T(8,128)(2,1)} %get-tuple-element.449, f32[720,128]{1,0:T(8,128)} %get-tuple-element.344, f32[9]{0:T(128)S(1)} %get-tuple-element.345, f32[720,128]{1,0:T(8,128)} %get-tuple-element.346, ...), kind=kOutput, calls=%fused_computation.53.clone.1 | convolution fusion | flops 237219840 | bytes 6194204 | tf_op jit(solution)/shard_map/while/body/eval_jaxpr/kjc,kcd->jd/dot_general | solution.py:61
  370.3 7.1 %fusion.142 = f32[12,720,128]{2,1,0:T(8,128)} fusion(f32[12,720,128]{2,1,0:T(8,128)} %get-tuple-element.431, s32[]{:T(128)} %get-tuple-element.430, bf16[9,128,128]{2,1,0:T(8,128)(2,1)} %get-tuple-element.449, f32[720,128]{1,0:T(8,128)} %get-tuple-element.344, f32[9]{0:T(128)S(1)} %get-tuple-element.345, f32[720,128]{1,0:T(8,128)} %get-tuple-element.346, ...), kind=kOutput, calls=%fused_computation.53.clone.1 | convolution fusion | flops 237219840 | bytes 6194204 | tf_op jit(solution)/shard_map/while/body/eval_jaxpr/kjc,kcd->jd/dot_general | solution.py:61
  384.3 7.1 %fusion.142 = f32[12,720,128]{2,1,0:T(8,128)} fusion(f32[12,720,128]{2,1,0:T(8,128)} %get-tuple-element.431, s32[]{:T(128)} %get-tuple-element.430, bf16[9,128,128]{2,1,0:T(8,128)(2,1)} %get-tuple-element.449, f32[720,128]{1,0:T(8,128)} %get-tuple-element.344, f32[9]{0:T(128)S(1)} %get-tuple-element.345, f32[720,128]{1,0:T(8,128)} %get-tuple-element.346, ...), kind=kOutput, calls=%fused_computation.53.clone.1 | convolution fusion | flops 237219840 | bytes 6194204 | tf_op jit(solution)/shard_map/while/body/eval_jaxpr/kjc,kcd->jd/dot_general | solution.py:61
  398.2 7.1 %fusion.142 = f32[12,720,128]{2,1,0:T(8,128)} fusion(f32[12,720,128]{2,1,0:T(8,128)} %get-tuple-element.431, s32[]{:T(128)} %get-tuple-element.430, bf16[9,128,128]{2,1,0:T(8,128)(2,1)} %get-tuple-element.449, f32[720,128]{1,0:T(8,128)} %get-tuple-element.344, f32[9]{0:T(128)S(1)} %get-tuple-element.345, f32[720,128]{1,0:T(8,128)} %get-tuple-element.346, ...), kind=kOutput, calls=%fused_computation.53.clone.1 | convolution fusion | flops 237219840 | bytes 6194204 | tf_op jit(solution)/shard_map/while/body/eval_jaxpr/kjc,kcd->jd/dot_general | solution.py:61
  405.3 4.3 fusion.68
  411.1 20.5 %fusion.41 = bf16[8640,256]{1,0:T(8,128)(2,1)S(1)} fusion(bf16[8640,128]{1,0:T(8,128)(2,1)S(1)} %bitcast.341, bf16[2,128,256]{2,1,0:T(8,128)(2,1)S(1)} %copy-done.14), kind=kOutput, calls=%fused_computation.107 | convolution fusion | flops 710000640 | bytes 6701056 | tf_op jit(solution)/shard_map/dot_general | solution.py:73
  433.8 42.7 %all-gather = bf16[32,12,720]{2,1,0:T(8,128)(2,1)S(1)} all-gather(bf16[2,12,720]{2,1,0:T(8,128)(2,1)S(1)} %copy.27), channel_id=2, replica_groups=mesh['ens'=16,'space'=16] {'ens'}, dimensions={0}, use_global_device_ids=true | all-gather | bytes 587520 | tf_op jit(solution)/shard_map/all_gather | solution.py:119
  (177 shorter events, 137.4 us)
Async XLA Ops:
  0.6 432.2 %copy-start = (bf16[2,128]{1,0:T(2,128)(2,1)S(1)}, bf16[2,128]{1,0:T(2,128)(2,1)}, u32[]{:S(2)}) copy-start(bf16[2,128]{1,0:T(2,128)(2,1)} %param.21) | copy-start | bytes 1540
  0.6 14.9 %copy-start.12 = (s32[192]{0:T(256)S(1)}, s32[192]{0:T(256)}, u32[]{:S(2)}) copy-start(s32[192]{0:T(256)} %param.22) | copy-start | bytes 2308
  2.0 20.0 %copy-start.3 = (bf16[2,9,128,128]{3,2,1,0:T(8,128)(2,1)S(1)}, bf16[2,9,128,128]{3,2,1,0:T(8,128)(2,1)}, u32[]{:S(2)}) copy-start(bf16[2,9,128,128]{3,2,1,0:T(8,128)(2,1)} %param.16) | copy-start | bytes 1769476
  9.0 13.9 %collective-permute-start = (bf16[1,2,720,128]{3,2,1,0:T(8,128)(2,1)}, bf16[1,2,720,128]{3,2,1,0:T(8,128)(2,1)S(1)}, u32[]{:S(2)}, u32[]{:S(2)}) collective-permute-start(bf16[1,2,720,128]{3,2,1,0:T(8,128)(2,1)} %get-tuple-element.166), channel_id=1, source_target_pairs={{0,1},{1,2},{2,3},{3,4},{4,5},{5,6},{6,7},{7,8},{8,9},{9,10},{10,1... | collective-permute-start | bytes 1105928 | tf_op jit(solution)/shard_map/ppermute | solution.py:20
  13.6 9.3 %collective-permute-start.1 = (bf16[1,2,720,128]{3,2,1,0:T(8,128)(2,1)S(1)}, bf16[1,2,720,128]{3,2,1,0:T(8,128)(2,1)}, u32[]{:S(2)}, u32[]{:S(2)}) collective-permute-start(bf16[1,2,720,128]{3,2,1,0:T(8,128)(2,1)S(1)} %get-tuple-element.167), channel_id=1, source_target_pairs={{1,0},{2,1},{3,2},{4,3},{5,4},{6,5},{7,6},{8,7},{9,8},{10,9},{11,1... | collective-permute-start | bytes 1105928 | tf_op jit(solution)/shard_map/ppermute | solution.py:21
  15.7 9.4 %copy-start.7 = (s32[4,12]{0,1:T(8,128)}, s32[4,12]{0,1:T(8,128)S(1)}, u32[]{:S(2)}) copy-start(s32[4,12]{0,1:T(8,128)S(1)} %iota_add_fusion) | copy-start | bytes 580
  19.7 0.6 copy-start.10
  190.2 4.3 copy-start.9
  194.5 1.5 copy-start.13
  196.0 20.5 %copy-start.5 = (bf16[2,256,128]{2,1,0:T(8,128)(2,1)S(1)}, bf16[2,256,128]{2,1,0:T(8,128)(2,1)}, u32[]{:S(2)}) copy-start(bf16[2,256,128]{2,1,0:T(8,128)(2,1)} %param.20) | copy-start | bytes 393220
  218.0 1.4 copy-start.2
  218.0 9.3 %copy-start.4 = (bf16[1,9,4,3,12]{4,2,3,1,0:T(4,128)(2,1)S(1)}, bf16[1,9,4,3,12]{4,2,3,1,0:T(4,128)(2,1)}, u32[]{:S(2)}) copy-start(bf16[1,9,4,3,12]{4,2,3,1,0:T(4,128)(2,1)} %get-tuple-element.178) | copy-start | bytes 7780
  218.0 9.5 %copy-start.6 = (f32[2,12,45]{2,0,1:T(2,128)S(1)}, f32[2,12,45]{2,0,1:T(2,128)}, u32[]{:S(2)}) copy-start(f32[2,12,45]{2,0,1:T(2,128)} %param.15) | copy-start | bytes 12964
  218.0 9.5 %copy-start.11 = (pred[4,12]{0,1:T(8,128)(4,1)S(1)}, pred[4,12]{0,1:T(8,128)(4,1)}, u32[]{:S(2)}) copy-start(pred[4,12]{0,1:T(8,128)(4,1)} %copy-done.10) | copy-start | bytes 148
  221.6 8.4 %collective-permute-start.2 = (bf16[1,2,720,128]{3,2,1,0:T(8,128)(2,1)}, bf16[1,2,720,128]{3,2,1,0:T(8,128)(2,1)S(1)}, u32[]{:S(2)}, u32[]{:S(2)}) collective-permute-start(bf16[1,2,720,128]{3,2,1,0:T(8,128)(2,1)} %get-tuple-element.164), channel_id=1, source_target_pairs={{0,1},{1,2},{2,3},{3,4},{4,5},{5,6},{6,7},{7,8},{8,9},{9,10},{10,1... | collective-permute-start | bytes 1105928 | tf_op jit(solution)/shard_map/ppermute | solution.py:20
  225.2 8.8 %collective-permute-start.3 = (bf16[1,2,720,128]{3,2,1,0:T(8,128)(2,1)S(1)}, bf16[1,2,720,128]{3,2,1,0:T(8,128)(2,1)S(1)}, u32[]{:S(2)}, u32[]{:S(2)}) collective-permute-start(bf16[1,2,720,128]{3,2,1,0:T(8,128)(2,1)S(1)} %get-tuple-element.165), channel_id=1, source_target_pairs={{1,0},{2,1},{3,2},{4,3},{5,4},{6,5},{7,6},{8,7},{9,8},{10,9},{11,1... | collective-permute-start | bytes 1105928 | tf_op jit(solution)/shard_map/ppermute | solution.py:21
  405.3 4.3 copy-start.8
  409.6 1.5 copy-start.14
  432.9 45.0 %copy-start.1 = (bf16[1,12,720,128]{3,2,1,0:T(8,128)(2,1)}, bf16[1,12,720,128]{3,2,1,0:T(8,128)(2,1)S(1)}, u32[]{:S(2)}) copy-start(bf16[1,12,720,128]{3,2,1,0:T(8,128)(2,1)S(1)} %fusion.71) | copy-start | bytes 6635524
where the time goes:
time: 487 us; the launch traced here: 478 us
  matrix products  218 us (45%)
  other arithmetic  97 us (20%)
  loops' own time  73.1 us (15%)
  blocking collectives  42.7 us (9%)
  local copies, waits for them, and re-layouts  29.3 us (6%)
  starting transfers between devices  12.2 us (3%)
    dot_general x24, matrix products, one_row(): jnp.einsum('kjc,kcd->jd', gathered, mixing_weight, preferred_element_type...  170 us
    another operation x2, loops' own time, disco_rows(): return lax.map(one_row, jnp.arange(row_count, dtype=jnp.int32))  73.1 us
    mul x24, other arithmetic, one_row(): row_weights[:, shift, lat_offset][:, None, None] * source[None]  57 us
    all_gather x1, blocking collectives, body(): lax.all_gather(lowest_level_prediction.astype(jnp.bfloat16), 'ens', axis=...  42.7 us
    dot_general x2, matrix products, block_tail(): jnp.dot(normed.reshape(-1, channels), up_matrix, preferred_element_type=j...  40.9 us
    convert_element_type x24, other arithmetic, one_row(): lax.dynamic_index_in_dim(bands, row, 2, keepdims=False).astype(jnp.float32)  16.8 us
    dynamic_slice x24, local copies, waits for them, and re-layouts, disco_rows(): return lax.map(one_row, jnp.arange(row_count, dtype=jnp.int32))  13.8 us
    reduce_sum x3, other arithmetic, normalize(): jnp.mean(widened * widened, axis=-1, keepdims=True) + 1e-06  11.5 us
  transfers between devices with their start and end apart: 4, of which 2 were waited for; matrix products, arithmetic and copies ran while one was open for 2% of the time, Pallas kernels for 0%

commit v1 on v0

v1 whole, which is shorter than its diff:
```python
import jax
import jax.numpy as jnp
from jax import lax
from jax.experimental import pallas as pl
from jax.experimental.pallas import tpu as pltpu
from jax.sharding import PartitionSpec as P

K = 9
BMAX = 4
HALO = 2
LW = 3
BLOCKS = 2
ROWS = 12
LON = 720
PAIRS = 368
C = 128
STEP = 80
PARTS = ((0, 192), (192, 176))
f32 = jnp.float32
bf16 = jnp.bfloat16


def unit(v, gain):
    return v * lax.rsqrt(jnp.mean(v * v, axis=-1, keepdims=True) + 1e-6) * gain


def prep_row(x, gain, a, s, nrm, raw):
    for t in range(0, LON, STEP):
        v = x[pl.ds(t, STEP), :].astype(f32)
        nrm[pl.ds(8 + t, STEP), :] = unit(v, gain)
        if s is not None:
            raw[pl.ds(t, STEP), :] = v
    nrm[7:8, :] = nrm[727:728, :]
    nrm[728:729, :] = nrm[8:9, :]
    for j in range(4):
        a[:, j * C : (j + 1) * C] = nrm[pl.ds(7 + j, PAIRS, stride=2), :].astype(bf16)
    if s is not None:
        for j in range(2):
            s[:, j * C : (j + 1) * C] = raw[pl.ds(j, PAIRS, stride=2), :].astype(bf16)


def make_taps(band, mix, mx, wf, taps):
    mx[...] = jnp.zeros_like(mx)
    for k in range(K):
        mx[pl.ds(k, C, stride=16), :] = mix[k].astype(f32)
    coef = band[...]

    def channels(i, carry):
        for u in range(4):
            c = i * 4 + u
            rhs = jnp.concatenate(
                [mx[pl.ds(c * 32, 16), :], mx[pl.ds(c * 32 + 16, 16), :]], axis=1
            ).astype(bf16)
            out = jnp.dot(coef, rhs, preferred_element_type=f32)
            wf[pl.ds(c * 288, 144), :] = out[:, :C]
            wf[pl.ds(c * 288 + 144, 144), :] = out[:, C:]
        return carry

    lax.fori_loop(0, 16, channels, 0)

    def place(i, carry):
        for l in range(LW):
            w = wf[pl.ds(i * LW + l, C, stride=144), :].astype(bf16)
            taps[i, l * C : (l + 1) * C, 0:C] = w
            taps[i, (l + 1) * C : (l + 2) * C, C : 2 * C] = w
        taps[i, 3 * C : 4 * C, 0:C] = jnp.zeros((C, C), bf16)
        taps[i, 0:C, C : 2 * C] = jnp.zeros((C, C), bf16)
        return carry

    lax.fori_loop(0, ROWS * BMAX, place, 0)


def conv_row(o, start, a, s, taps, car):
    rows = [jnp.clip(start[o] + q, 0, ROWS + 2 * HALO - 1) for q in range(BMAX)]
    for p, n in PARTS:
        acc = jnp.dot(a[rows[0], pl.ds(p, n), :], taps[o * BMAX], preferred_element_type=f32)
        for q in range(1, BMAX):
            acc += jnp.dot(
                a[rows[q], pl.ds(p, n), :], taps[o * BMAX + q], preferred_element_type=f32
            )
        car[pl.ds(p, n), :] = (s[o, pl.ds(p, n), :].astype(f32) + acc).astype(bf16).astype(f32)


def mlp_row(gain, up, down, car, emit):
    for p, n in PARTS:
        rest = jnp.concatenate([car[pl.ds(p, n), :C], car[pl.ds(p, n), C:]], axis=0)
        h = jnp.dot(unit(rest, gain).astype(bf16), up, preferred_element_type=f32)
        h = (0.5 * h * (1.0 + lax.erf(h * 0.7071067811865476))).astype(bf16)
        y = rest + jnp.dot(h, down, preferred_element_type=f32)
        emit(p, n, y[:n], y[n:])


def block_kernel(
    start, x, before, after, band, mix, gains, up, down, out, a, s, taps, nrm, raw, fin, mx, wf, car
):
    make_taps(band, mix, mx, wf, taps)
    gain = gains[0:1]

    def prep(i, carry):
        prep_row(x.at[i], gain, a.at[i + HALO], s.at[i], nrm, raw)
        return carry

    lax.fori_loop(0, ROWS, prep, 0)
    for i in range(HALO):
        prep_row(before.at[i], gain, a.at[i], None, nrm, raw)
        prep_row(after.at[i], gain, a.at[ROWS + HALO + i], None, nrm, raw)
    gain2 = gains[1:2]
    up_matrix, down_matrix = up[...], down[...]

    def row(o, carry):
        def emit(p, n, even, odd):
            fin[pl.ds(2 * p, n, stride=2), :] = even
            fin[pl.ds(2 * p + 1, n, stride=2), :] = odd

        conv_row(o, start, a, s, taps, car)
        mlp_row(gain2, up_matrix, down_matrix, car, emit)
        out[o] = fin[0:LON, :].astype(bf16)
        return carry

    lax.fori_loop(0, ROWS, row, 0)


def block(start, x, before, after, band, mix, gains, up, down):
    vmem = pl.BlockSpec(memory_space=pltpu.VMEM)
    return pl.pallas_call(
        block_kernel,
        out_shape=jax.ShapeDtypeStruct(x.shape, bf16),
        in_specs=[pl.BlockSpec(memory_space=pltpu.SMEM)] + [vmem] * 8,
        out_specs=vmem,
        scratch_shapes=[
            pltpu.VMEM((ROWS + 2 * HALO, PAIRS, 4 * C), bf16),
            pltpu.VMEM((ROWS, PAIRS, 2 * C), bf16),
            pltpu.VMEM((ROWS * BMAX, 4 * C, 2 * C), bf16),
            pltpu.VMEM((752, C), f32),
            pltpu.VMEM((2 * PAIRS, C), f32),
            pltpu.VMEM((2 * PAIRS, C), f32),
            pltpu.VMEM((16 * C, C), f32),
            pltpu.VMEM((144 * C, C), f32),
            pltpu.VMEM((PAIRS, 2 * C), f32),
        ],
        compiler_params=pltpu.CompilerParams(vmem_limit_bytes=56 * 2**20),
    )(start, x, before, after, band, mix, gains, up, down)


def band_taps(basis_coef, local_width, row_first):
    coef = lax.dynamic_slice_in_dim(basis_coef, row_first, ROWS, axis=4)
    inside = jnp.arange(BMAX, dtype=jnp.int32)[:, None] < local_width[None, :]
    coef = jnp.where(inside[None, None, :, None, :], coef, jnp.zeros_like(coef))
    coef = coef.transpose(0, 4, 2, 3, 1).reshape(BLOCKS, ROWS * BMAX * LW, K)
    return jnp.pad(coef, ((0, 0), (0, 0), (0, 16 - K)))


def body(
    hidden_vectors,
    target,
    mix_weight,
    basis_coef,
    rescaling_factors,
    up_weight,
    down_weight,
    readout_matrix,
    band_start,
    band_width,
):
    row_first = lax.axis_index("space") * ROWS
    local_start = lax.dynamic_slice_in_dim(band_start, row_first, ROWS)
    local_width = lax.dynamic_slice_in_dim(band_width, row_first, ROWS)
    start = local_start - row_first + HALO
    bands = band_taps(basis_coef, local_width, row_first)
    peers = lax.axis_size("space")
    forward = [(i, i + 1) for i in range(peers - 1)]
    backward = [(j, i) for i, j in forward]
    x = hidden_vectors[0]
    for b in range(BLOCKS):
        before = lax.ppermute(x[ROWS - HALO :], "space", forward)
        after = lax.ppermute(x[:HALO], "space", backward)
        x = block(
            start,
            x,
            before,
            after,
            bands[b],
            mix_weight[b],
            rescaling_factors[b],
            up_weight[b],
            down_weight[b],
        )
    state = x[None]
    surface = jnp.einsum("uzgm,wm->uwzg", state, readout_matrix, preferred_element_type=f32)
    lon_cols = target.shape[2]
    everyone = lax.all_gather(surface.astype(bf16), "ens", axis=0, tiled=True).astype(f32)
    members = lax.dynamic_slice_in_dim(
        everyone, lax.axis_index("ens") * lon_cols, lon_cols, axis=3
    )
    count = members.shape[0]
    skill = jnp.mean(jnp.abs(members - target[None]), axis=0)
    spread = jnp.sum(jnp.abs(members[:, None] - members[None]), axis=(0, 1))
    return (state, skill - spread / (2.0 * count * (count - 1)))


def solution(mesh):
    in_specs = (P("ens", "space", None, None), P(None, "space", "ens")) + (P(),) * 8
    out_specs = (P("ens", "space", None, None), P(None, "space", "ens"))
    return jax.shard_map(body, mesh=mesh, in_specs=in_specs, out_specs=out_specs, check_vma=False)
```

time: 487 us -> 147 us (0.30)
  the two profiles are of different devices: /device:TPU:1 before, /device:TPU:14 now
where the time goes in v1:
time: 147 us; the launch traced here: 146 us
  Pallas kernels  61 us (41%)
  blocking collectives  49.5 us (34%)
  local copies, waits for them, and re-layouts  11.6 us (8%)
  starting transfers between devices  11.1 us (8%)
  waiting for transfers between devices  6.95 us (5%)
  other arithmetic  2.86 us (2%)
  matrix products  2.47 us (2%)
    pallas_call x2, Pallas kernels, block(): pl.pallas_call(block_kernel, out_shape=jax.ShapeDtypeStruct(x.shape, bf16...  61 us
    all_gather x1, blocking collectives, body(): lax.all_gather(surface.astype(bf16), 'ens', axis=0, tiled=True).astype(f32)  49.5 us
    ppermute x2, starting transfers between devices, body(): after = lax.ppermute(x[:HALO], 'space', backward)  7.28 us
    ppermute x2, starting transfers between devices, body(): before = lax.ppermute(x[ROWS - HALO:], 'space', forward)  3.84 us
    ppermute x2, waiting for transfers between devices, body(): after = lax.ppermute(x[:HALO], 'space', backward)  3.72 us
    ppermute x2, waiting for transfers between devices, body(): before = lax.ppermute(x[ROWS - HALO:], 'space', forward)  3.23 us
  transfers between devices with their start and end apart: 4, of which 2 were waited for; matrix products, arithmetic and copies ran while one was open for 6% of the time, Pallas kernels for 0%

profile of v1, /device:TPU:14, one launch (start us, length us, event | category | flops | bytes accessed | tf_op | source)
XLA Modules:
  0.0 146.3 jit_solution(7233231174706785436)
XLA Ops:
  0.6 0.0 copy-start
  0.7 1.2 slice_bitcast_fusion
  1.9 1.9 %collective-permute-start = (bf16[2,720,128]{2,1,0:T(8,128)(2,1)S(1)}, bf16[2,720,128]{2,1,0:T(8,128)(2,1)S(1)}, u32[]{:S(2)}, u32[]{:S(2)}) collective-permute-start(bf16[2,720,128]{2,1,0:T(8,128)(2,1)S(1)} %get-tuple-element.9), channel_id=1, source_target_pairs={{0,1},{1,2},{2,3},{3,4},{4,5},{5,6},{6,7},{7,8},{8,9},{9,10},{10,1... | collective-permute-start | bytes 1105928 | tf_op jit(solution)/shard_map/ppermute | solution.py:175
  3.8 3.6 %collective-permute-start.1 = (bf16[2,720,128]{2,1,0:T(8,128)(2,1)S(1)}, bf16[2,720,128]{2,1,0:T(8,128)(2,1)S(1)}, u32[]{:S(2)}, u32[]{:S(2)}) collective-permute-start(bf16[2,720,128]{2,1,0:T(8,128)(2,1)S(1)} %get-tuple-element.8), channel_id=1, source_target_pairs={{1,0},{2,1},{3,2},{4,3},{5,4},{6,5},{7,6},{8,7},{9,8},{10,9},{11,1... | collective-permute-start | bytes 1105928 | tf_op jit(solution)/shard_map/ppermute | solution.py:176
  7.5 0.8 dynamic_slice.13
  8.2 1.6 %slice_bitcast_fusion.4 = (bf16[256,128]{1,0:T(8,128)(2,1)}, bf16[256,128]{1,0:T(8,128)(2,1)}) fusion(bf16[2,256,128]{2,1,0:T(8,128)(2,1)} %param.16), kind=kLoop, calls=%fused_computation.9 | loop fusion | bytes 262144 | tf_op jit(solution)/shard_map/squeeze | solution.py:186
  9.8 1.5 %slice_bitcast_fusion.5 = (bf16[128,256]{1,0:T(8,128)(2,1)}, bf16[128,256]{1,0:T(8,128)(2,1)}) fusion(bf16[2,128,256]{2,1,0:T(8,128)(2,1)} %param.15), kind=kLoop, calls=%fused_computation.10 | loop fusion | bytes 262144 | tf_op jit(solution)/shard_map/squeeze | solution.py:185
  11.3 1.3 slice_bitcast_fusion.8
  12.6 0.9 select_bitcast_fusion
  13.5 1.2 subtract_add_fusion.start
  14.7 0.3 copy.28
  15.0 0.6 fusion.2
  15.6 0.9 slice_bitcast_fusion.2
  16.5 0.0 collective-permute-done.before
  16.5 0.0 collective-permute-done.1.after
  16.5 0.7 copy-done.2
  17.3 0.1 copy-done.3
  17.4 30.5 %shard_map.113.x = bf16[12,720,128]{2,1,0:T(8,128)(2,1)} custom-call(s32[12]{0:T(128)} %subtract_add_fusion.start, bf16[12,720,128]{2,1,0:T(8,128)(2,1)} %bitcast.38, bf16[2,720,128]{2,1,0:T(8,128)(2,1)} %copy-done.2, bf16[2,720,128]{2,1,0:T(8,128)(2,1)} %copy-done.3, bf16[144,16]{1,0:T(8,128)(2,1)} %get-tuple-element.17.band, ...), custom_call_target="tpu_custom_call" | custom-call | tf_op jit(solution)/shard_map/pallas_call | solution.py:125
  47.9 1.1 fusion.4
  49.0 1.9 %collective-permute-start.2 = (bf16[2,720,128]{2,1,0:T(8,128)(2,1)S(1)}, bf16[2,720,128]{2,1,0:T(8,128)(2,1)S(1)}, u32[]{:S(2)}, u32[]{:S(2)}) collective-permute-start(bf16[2,720,128]{2,1,0:T(8,128)(2,1)S(1)} %get-tuple-element.7), channel_id=1, source_target_pairs={{0,1},{1,2},{2,3},{3,4},{4,5},{5,6},{6,7},{7,8},{8,9},{9,10},{10,1... | collective-permute-start | bytes 1105928 | tf_op jit(solution)/shard_map/ppermute | solution.py:175
  51.0 3.6 %collective-permute-start.3 = (bf16[2,720,128]{2,1,0:T(8,128)(2,1)S(1)}, bf16[2,720,128]{2,1,0:T(8,128)(2,1)S(1)}, u32[]{:S(2)}, u32[]{:S(2)}) collective-permute-start(bf16[2,720,128]{2,1,0:T(8,128)(2,1)S(1)} %get-tuple-element.6), channel_id=1, source_target_pairs={{1,0},{2,1},{3,2},{4,3},{5,4},{6,5},{7,6},{8,7},{9,8},{10,9},{11,1... | collective-permute-start | bytes 1105928 | tf_op jit(solution)/shard_map/ppermute | solution.py:176
  54.6 3.2 %collective-permute-done.2.before = bf16[2,720,128]{2,1,0:T(8,128)(2,1)S(1)} collective-permute-done((bf16[2,720,128]{2,1,0:T(8,128)(2,1)S(1)}, bf16[2,720,128]{2,1,0:T(8,128)(2,1)S(1)}, u32[]{:S(2)}, u32[]{:S(2)}) %collective-permute-start.2) | collective-permute-done | bytes 368672 | tf_op jit(solution)/shard_map/ppermute | solution.py:175
  57.9 3.7 %collective-permute-done.3.after = bf16[2,720,128]{2,1,0:T(8,128)(2,1)S(1)} collective-permute-done((bf16[2,720,128]{2,1,0:T(8,128)(2,1)S(1)}, bf16[2,720,128]{2,1,0:T(8,128)(2,1)S(1)}, u32[]{:S(2)}, u32[]{:S(2)}) %collective-permute-start.3) | collective-permute-done | bytes 368672 | tf_op jit(solution)/shard_map/ppermute | solution.py:176
  61.6 0.8 copy-done.5
  62.3 30.5 %shard_map.114 = bf16[12,720,128]{2,1,0:T(8,128)(2,1)} custom-call(s32[12]{0:T(128)} %subtract_add_fusion.start, bf16[12,720,128]{2,1,0:T(8,128)(2,1)} %shard_map.113.x, bf16[2,720,128]{2,1,0:T(8,128)(2,1)} %copy-done.4, bf16[2,720,128]{2,1,0:T(8,128)(2,1)} %copy-done.5, bf16[144,16]{1,0:T(8,128)(2,1)} %get-tuple-element.16.band, ...), custom_call_target="tpu_custom_call" | custom-call | tf_op jit(solution)/shard_map/pallas_call | solution.py:125
  92.8 2.5 %fusion = bf16[2,12,720]{2,0,1:T(2,128)(2,1)S(1)} fusion(bf16[12,720,128]{2,1,0:T(8,128)(2,1)} %shard_map.114, bf16[2,128]{1,0:T(2,128)(2,1)S(1)} %copy-done), kind=kOutput, calls=%fused_computation.2 | convolution fusion | flops 4440960 | bytes 2246912 | tf_op jit(solution)/shard_map/uzgm,wm->uwzg/dot_general | solution.py:189
  95.3 49.5 %all-gather = bf16[32,12,720]{2,1,0:T(8,128)(2,1)S(1)} all-gather(bf16[2,12,720]{2,1,0:T(8,128)(2,1)S(1)} %copy.30), channel_id=2, replica_groups=mesh['ens'=16,'space'=16] {'ens'}, dimensions={0}, use_global_device_ids=true | all-gather | bytes 587520 | tf_op jit(solution)/shard_map/all_gather | solution.py:191
  144.9 0.1 dynamic-slice_convert_fusion
  145.0 0.1 copy.32
  145.1 0.4 abs_reduce_fusion
  145.5 0.1 abs_reduce_fusion.1
  145.7 0.6 copy.33
  (15 shorter events, 0.1 us)
Async XLA Ops:
  0.6 92.2 %copy-start = (bf16[2,128]{1,0:T(2,128)(2,1)S(1)}, bf16[2,128]{1,0:T(2,128)(2,1)}, u32[]{:S(2)}) copy-start(bf16[2,128]{1,0:T(2,128)(2,1)} %param.17) | copy-start | bytes 1540
  0.6 15.0 %copy-start.1 = (bf16[2,9,128,128]{3,2,1,0:T(8,128)(2,1)S(1)}, bf16[2,9,128,128]{3,2,1,0:T(8,128)(2,1)}, u32[]{:S(2)}) copy-start(bf16[2,9,128,128]{3,2,1,0:T(8,128)(2,1)} %param.12) | copy-start | bytes 1769476
  1.9 14.7 %collective-permute-start = (bf16[2,720,128]{2,1,0:T(8,128)(2,1)S(1)}, bf16[2,720,128]{2,1,0:T(8,128)(2,1)S(1)}, u32[]{:S(2)}, u32[]{:S(2)}) collective-permute-start(bf16[2,720,128]{2,1,0:T(8,128)(2,1)S(1)} %get-tuple-element.9), channel_id=1, source_target_pairs={{0,1},{1,2},{2,3},{3,4},{4,5},{5,6},{6,7},{7,8},{8,9},{9,10},{10,1... | collective-permute-start | bytes 1105928 | tf_op jit(solution)/shard_map/ppermute | solution.py:175
  3.8 12.7 %collective-permute-start.1 = (bf16[2,720,128]{2,1,0:T(8,128)(2,1)S(1)}, bf16[2,720,128]{2,1,0:T(8,128)(2,1)S(1)}, u32[]{:S(2)}, u32[]{:S(2)}) collective-permute-start(bf16[2,720,128]{2,1,0:T(8,128)(2,1)S(1)} %get-tuple-element.8), channel_id=1, source_target_pairs={{1,0},{2,1},{3,2},{4,3},{5,4},{6,5},{7,6},{8,7},{9,8},{10,9},{11,1... | collective-permute-start | bytes 1105928 | tf_op jit(solution)/shard_map/ppermute | solution.py:176
  16.5 0.7 copy-start.2
  16.5 0.9 copy-start.3
  17.4 37.2 %copy-start.6 = (f32[2,12,45]{2,0,1:T(2,128)S(1)}, f32[2,12,45]{2,0,1:T(2,128)}, u32[]{:S(2)}) copy-start(f32[2,12,45]{2,0,1:T(2,128)} %param.11) | copy-start | bytes 12964
  49.0 8.8 %collective-permute-start.2 = (bf16[2,720,128]{2,1,0:T(8,128)(2,1)S(1)}, bf16[2,720,128]{2,1,0:T(8,128)(2,1)S(1)}, u32[]{:S(2)}, u32[]{:S(2)}) collective-permute-start(bf16[2,720,128]{2,1,0:T(8,128)(2,1)S(1)} %get-tuple-element.7), channel_id=1, source_target_pairs={{0,1},{1,2},{2,3},{3,4},{4,5},{5,6},{6,7},{7,8},{8,9},{9,10},{10,1... | collective-permute-start | bytes 1105928 | tf_op jit(solution)/shard_map/ppermute | solution.py:175
  51.0 10.6 %collective-permute-start.3 = (bf16[2,720,128]{2,1,0:T(8,128)(2,1)S(1)}, bf16[2,720,128]{2,1,0:T(8,128)(2,1)S(1)}, u32[]{:S(2)}, u32[]{:S(2)}) collective-permute-start(bf16[2,720,128]{2,1,0:T(8,128)(2,1)S(1)} %get-tuple-element.6), channel_id=1, source_target_pairs={{1,0},{2,1},{3,2},{4,3},{5,4},{6,5},{7,6},{8,7},{9,8},{10,9},{11,1... | collective-permute-start | bytes 1105928 | tf_op jit(solution)/shard_map/ppermute | solution.py:176
  57.9 3.7 %copy-start.4 = (bf16[2,720,128]{2,1,0:T(8,128)(2,1)}, bf16[2,720,128]{2,1,0:T(8,128)(2,1)S(1)}, u32[]{:S(2)}) copy-start(bf16[2,720,128]{2,1,0:T(8,128)(2,1)S(1)} %collective-permute-done.2.before) | copy-start | bytes 1105924
  61.6 0.8 copy-start.5

commit v2 on v1

v2 whole, which is shorter than its diff:
```python
import jax
import jax.numpy as jnp
from jax import lax
from jax.experimental import pallas as pl
from jax.experimental.pallas import tpu as pltpu
from jax.sharding import PartitionSpec as P

K = 9
BMAX = 4
HALO = 2
LW = 3
BLOCKS = 2
ROWS = 12
LON = 720
PAIRS = 368
C = 128
STEP = 80
PARTS = ((0, 192), (192, 176))
f32 = jnp.float32
bf16 = jnp.bfloat16
MESH = pl.DeviceIdType.MESH


def unit(v, gain):
    return v * lax.rsqrt(jnp.mean(v * v, axis=-1, keepdims=True) + 1e-6) * gain


def prep_row(x, gain, a, s, nrm, raw):
    for t in range(0, LON, STEP):
        v = x[pl.ds(t, STEP), :].astype(f32)
        nrm[pl.ds(8 + t, STEP), :] = unit(v, gain)
        if s is not None:
            raw[pl.ds(t, STEP), :] = v
    nrm[7:8, :] = nrm[727:728, :]
    nrm[728:729, :] = nrm[8:9, :]
    for j in range(4):
        a[:, j * C : (j + 1) * C] = nrm[pl.ds(7 + j, PAIRS, stride=2), :].astype(bf16)
    if s is not None:
        for j in range(2):
            s[:, j * C : (j + 1) * C] = raw[pl.ds(j, PAIRS, stride=2), :].astype(bf16)


def band_rows(b, me, basis, width, cf, bnd):
    lat = jax.lax.broadcasted_iota(jnp.int32, (16, 192), 1)
    own = jax.lax.broadcasted_iota(jnp.int32, (16, 192), 0)
    pick = jnp.where((lat == own + me * ROWS) & (own < ROWS), 1.0, 0.0).astype(bf16)
    row = jax.lax.broadcasted_iota(jnp.int32, (16, 16), 0)
    widths = jnp.zeros((16, 16), jnp.int32)
    for o in range(ROWS):
        widths = jnp.where(row == o, width[me * ROWS + o], widths)
    for k in range(K):
        for q in range(BMAX):
            v = basis[b, k, q].astype(f32)
            for l in range(LW):
                at = (q * LW + l) * 16 + k
                cf[at : at + 1, 0:192] = v[l : l + 1]
    for q in range(BMAX):
        for l in range(LW):
            at = q * LW + l
            part = lax.dot_general(
                pick,
                cf[at * 16 : at * 16 + 16, 0:192].astype(bf16),
                (((1,), (1,)), ((), ())),
                preferred_element_type=f32,
            )
            part = jnp.where(widths > q, part, 0.0)
            bnd[at * ROWS : at * ROWS + ROWS, 0:16] = part[:ROWS]


def make_taps(b, mix, mx, wf, bnd, taps):
    for k in range(K):
        mx[pl.ds(k, C, stride=16), :] = mix[b, k].astype(f32)
    coef = bnd[0:144, 0:16].astype(bf16)

    def channels(i, carry):
        for u in range(4):
            c = i * 4 + u
            rhs = jnp.concatenate(
                [mx[pl.ds(c * 32, 16), :], mx[pl.ds(c * 32 + 16, 16), :]], axis=1
            ).astype(bf16)
            out = jnp.dot(coef, rhs, preferred_element_type=f32)
            wf[pl.ds(c * 288, 144), :] = out[:, :C]
            wf[pl.ds(c * 288 + 144, 144), :] = out[:, C:]
        return carry

    lax.fori_loop(0, 16, channels, 0)

    def place(o, carry):
        for q in range(BMAX):
            i = o * BMAX + q
            for l in range(LW):
                w = wf[pl.ds((q * LW + l) * ROWS + o, C, stride=144), :].astype(bf16)
                taps[i, l * C : (l + 1) * C, 0:C] = w
                taps[i, (l + 1) * C : (l + 2) * C, C : 2 * C] = w
        return carry

    lax.fori_loop(0, ROWS, place, 0)


def prep_pairs(s, gain, a, even, odd):
    for p, n in PARTS:
        e = unit(s[pl.ds(p, n), 0:C].astype(f32), gain)
        o = unit(s[pl.ds(p, n), C : 2 * C].astype(f32), gain)
        a[pl.ds(p, n), C : 2 * C] = e.astype(bf16)
        a[pl.ds(p, n), 2 * C : 3 * C] = o.astype(bf16)
        even[pl.ds(8 + p, n), :] = e
        odd[pl.ds(8 + p, n), :] = o
    odd[7:8, :] = odd[367:368, :]
    even[368:369, :] = even[8:9, :]
    a[:, 0:C] = odd[7 : 7 + PAIRS, :].astype(bf16)
    a[:, 3 * C : 4 * C] = even[9 : 9 + PAIRS, :].astype(bf16)


def conv_row(o, start, first, a, s, taps, car):
    base = start[first + o] - first + HALO
    rows = [jnp.clip(base + q, 0, ROWS + 2 * HALO - 1) for q in range(BMAX)]
    for p, n in PARTS:
        acc = jnp.dot(a[rows[0], pl.ds(p, n), :], taps[o * BMAX], preferred_element_type=f32)
        for q in range(1, BMAX):
            acc += jnp.dot(
                a[rows[q], pl.ds(p, n), :], taps[o * BMAX + q], preferred_element_type=f32
            )
        car[pl.ds(p, n), :] = (s[o, pl.ds(p, n), :].astype(f32) + acc).astype(bf16).astype(f32)


def mlp_row(gain, up, down, car, emit):
    for p, n in PARTS:
        rest = jnp.concatenate([car[pl.ds(p, n), :C], car[pl.ds(p, n), C:]], axis=0)
        h = jnp.dot(unit(rest, gain).astype(bf16), up, preferred_element_type=f32)
        h = (0.5 * h * (1.0 + lax.erf(h * 0.7071067811865476))).astype(bf16)
        y = rest + jnp.dot(h, down, preferred_element_type=f32)
        emit(p, n, y[:n], y[n:])


def both(first, second):
    lane = jax.lax.broadcasted_iota(jnp.int32, first.shape, 1)
    return jnp.where(lane < 64, first, pltpu.roll(second, 64, 1))


def step_kernel(
    start, width, x, target, mix, basis, gains, up, down, readout,
    out, score,
    xv, ov, a, s, taps, nrm, raw, fin, mx, wf, car, cf, bnd, even, odd,
    halo0, halo1, surf, tgt, snd, rcv,
    x_sem, out_sem, send_sem, recv_sem, ens_send, ens_recv,
):
    me = lax.axis_index("space")
    ens = lax.axis_index("ens")
    members = rcv.shape[0]
    last = lax.axis_size("space") - 1
    barrier = pltpu.get_barrier_semaphore()
    for step in range(1, members):
        pl.semaphore_signal(
            barrier, inc=1, device_id={"ens": lax.rem(ens + step, members)}, device_id_type=MESH
        )

    @pl.when(me > 0)
    def _():
        pl.semaphore_signal(barrier, inc=1, device_id={"space": me - 1}, device_id_type=MESH)

    @pl.when(me < last)
    def _():
        pl.semaphore_signal(barrier, inc=1, device_id={"space": me + 1}, device_id_type=MESH)

    x_copy = pltpu.make_async_copy(x.at[0], xv, x_sem)
    x_copy.start()
    mx[...] = jnp.zeros_like(mx)
    cf[...] = jnp.zeros_like(cf)

    def clear(i, carry):
        taps[i, 3 * C : 4 * C, 0:C] = jnp.zeros((C, C), bf16)
        taps[i, 0:C, C : 2 * C] = jnp.zeros((C, C), bf16)
        return carry

    lax.fori_loop(0, ROWS * BMAX, clear, 0)
    for i in range(HALO):
        a[i] = jnp.zeros((PAIRS, 4 * C), bf16)
        a[ROWS + HALO + i] = jnp.zeros((PAIRS, 4 * C), bf16)
    band_rows(0, me, basis, width, cf, bnd)
    make_taps(0, mix, mx, wf, bnd, taps)

    middle = (me > 0) & (me < last)

    @pl.when(middle)
    def _():
        pl.semaphore_wait(barrier, members + 1)

    @pl.when(jnp.logical_not(middle))
    def _():
        pl.semaphore_wait(barrier, members)

    def forward(b):
        source, landing = (x.at[0], halo0) if b == 0 else (s, halo1)
        return pltpu.make_async_remote_copy(
            src_ref=source.at[pl.ds(ROWS - HALO, HALO)],
            dst_ref=landing.at[pl.ds(0, HALO)],
            send_sem=send_sem.at[b, 0],
            recv_sem=recv_sem.at[b, 0],
            device_id={"space": me + 1},
            device_id_type=MESH,
        )

    def backward(b):
        source, landing = (x.at[0], halo0) if b == 0 else (s, halo1)
        return pltpu.make_async_remote_copy(
            src_ref=source.at[pl.ds(0, HALO)],
            dst_ref=landing.at[pl.ds(HALO, HALO)],
            send_sem=send_sem.at[b, 1],
            recv_sem=recv_sem.at[b, 1],
            device_id={"space": me - 1},
            device_id_type=MESH,
        )

    def send_forward(b):
        @pl.when(me < last)
        def _():
            forward(b).start()

    def send_backward(b):
        @pl.when(me > 0)
        def _():
            backward(b).start()

    send_forward(0)
    send_backward(0)
    first = me * ROWS

    def halo_rows(b, side):
        def fill(i, carry):
            at = side * HALO + i
            row = a.at[side * (ROWS + HALO) + i]
            if b == 0:
                prep_row(halo0.at[at], gains[0, 0:1], row, None, nrm, raw)
            else:
                prep_pairs(halo1.at[at], gains[1, 0:1], row, even, odd)
            return carry

        def empty():
            for i in range(HALO):
                a[side * (ROWS + HALO) + i] = jnp.zeros((PAIRS, 4 * C), bf16)

        has = me > 0 if side == 0 else me < last

        @pl.when(has)
        def _():
            (forward(b) if side == 0 else backward(b)).wait_recv()
            lax.fori_loop(0, HALO, fill, 0)

        @pl.when(jnp.logical_not(has))
        def _():
            empty()

    lead = jnp.concatenate([readout[...].astype(f32), jnp.zeros((14, C), f32)], axis=0).astype(bf16)

    def rows(b, low, high):
        gain2 = gains[b, 1:2]
        up_matrix, down_matrix = up[b], down[b]

        def row(o, carry):
            def emit(p, n, e, d):
                if b == 0:
                    s[o, pl.ds(p, n), 0:C] = e.astype(bf16)
                    s[o, pl.ds(p, n), C : 2 * C] = d.astype(bf16)
                else:
                    fin[pl.ds(2 * p, n, stride=2), :] = e
                    fin[pl.ds(2 * p + 1, n, stride=2), :] = d

            conv_row(o, start, first, a, s, taps, car)
            mlp_row(gain2, up_matrix, down_matrix, car, emit)
            if b == 1:
                state = fin[0:LON, :].astype(bf16)
                ov[o] = state
                pltpu.make_async_copy(ov.at[o], out.at[0, o], out_sem.at[o]).start()
                seen = lax.dot_general(
                    lead, state, (((1,), (1,)), ((), ())), preferred_element_type=f32
                )
                surf[pl.ds(o, 1), 0:LON] = seen[0:1]
                surf[pl.ds(16 + o, 1), 0:LON] = seen[1:2]
            return carry

        lax.fori_loop(low, high, row, 0)

    x_copy.wait()

    def prep0(i, carry):
        prep_row(xv.at[i], gains[0, 0:1], a.at[i + HALO], s.at[i], nrm, raw)
        return carry

    lax.fori_loop(0, ROWS, prep0, 0)
    rows(0, HALO, ROWS - HALO)
    halo_rows(0, 0)
    rows(0, 0, HALO)
    send_backward(1)
    halo_rows(0, 1)
    rows(0, ROWS - HALO, ROWS)
    send_forward(1)

    band_rows(1, me, basis, width, cf, bnd)
    make_taps(1, mix, mx, wf, bnd, taps)

    def prep1(i, carry):
        prep_pairs(s.at[i], gains[1, 0:1], a.at[i + HALO], even, odd)
        return carry

    lax.fori_loop(0, ROWS, prep1, 0)
    rows(1, HALO, ROWS - HALO)
    halo_rows(1, 0)
    rows(1, 0, HALO)
    halo_rows(1, 1)
    rows(1, ROWS - HALO, ROWS)

    cols = target.shape[2]
    for e in range(members):
        base = e * cols // 128 * 128
        turn = (256 - (e * cols - base)) % 256
        top = pltpu.roll(surf[0:16, base : base + 256], turn, 1)[:, 0:128]
        low = pltpu.roll(surf[16:32, base : base + 256], turn, 1)[:, 0:128]
        snd[e] = both(top, low).astype(bf16)
    rcv[ens] = snd[ens]

    def deal(step):
        peer = lax.rem(ens + step, members)
        return pltpu.make_async_remote_copy(
            src_ref=snd.at[peer],
            dst_ref=rcv.at[ens],
            send_sem=ens_send.at[step],
            recv_sem=ens_recv.at[ens],
            device_id={"ens": peer},
            device_id_type=MESH,
        )

    for step in range(1, members):
        deal(step).start()
    for v in range(2):
        tgt[v, 0:ROWS, 0:cols] = target[v]
    for step in range(1, members):
        peer = lax.rem(ens + step, members)
        pltpu.make_async_remote_copy(
            src_ref=snd.at[peer],
            dst_ref=rcv.at[peer],
            send_sem=ens_send.at[step],
            recv_sem=ens_recv.at[peer],
            device_id={"ens": peer},
            device_id_type=MESH,
        ).wait_recv()
    aim = both(tgt[0], tgt[1])
    field = [rcv[m].astype(f32) for m in range(members)]
    skill = sum(jnp.abs(f - aim) for f in field) * (1.0 / members)
    spread = jnp.zeros_like(aim)
    for m in range(members):
        for n in range(m):
            spread = spread + jnp.abs(field[m] - field[n])
    fair = skill - spread * (1.0 / (members * (members - 1)))
    score[0] = fair[0:ROWS, 0:cols]
    score[1] = pltpu.roll(fair, 64, 1)[0:ROWS, 0:cols]

    for step in range(1, members):
        deal(step).wait_send()
    for b in range(BLOCKS):

        @pl.when(me < last)
        def _():
            forward(b).wait_send()

        @pl.when(me > 0)
        def _():
            backward(b).wait_send()

    def finish(o, carry):
        pltpu.make_async_copy(ov.at[o], out.at[0, o], out_sem.at[o]).wait()
        return carry

    lax.fori_loop(0, ROWS, finish, 0)


def body(
    hidden_vectors, target, mix_weight, basis_coef, rescaling_factors,
    up_weight, down_weight, readout_matrix, band_start, band_width,
):
    members = lax.axis_size("ens")
    vmem = pl.BlockSpec(memory_space=pltpu.VMEM)
    smem = pl.BlockSpec(memory_space=pltpu.SMEM)
    return pl.pallas_call(
        step_kernel,
        out_shape=(
            jax.ShapeDtypeStruct(hidden_vectors.shape, bf16),
            jax.ShapeDtypeStruct(target.shape, f32),
        ),
        in_specs=[smem, smem, pl.BlockSpec(memory_space=pl.ANY)] + [vmem] * 7,
        out_specs=(pl.BlockSpec(memory_space=pl.ANY), vmem),
        scratch_shapes=[
            pltpu.VMEM((ROWS, LON, C), bf16),
            pltpu.VMEM((ROWS, LON, C), bf16),
            pltpu.VMEM((ROWS + 2 * HALO, PAIRS, 4 * C), bf16),
            pltpu.VMEM((ROWS, PAIRS, 2 * C), bf16),
            pltpu.VMEM((ROWS * BMAX, 4 * C, 2 * C), bf16),
            pltpu.VMEM((752, C), f32),
            pltpu.VMEM((2 * PAIRS, C), f32),
            pltpu.VMEM((2 * PAIRS, C), f32),
            pltpu.VMEM((16 * C, C), f32),
            pltpu.VMEM((144 * C, C), f32),
            pltpu.VMEM((PAIRS, 2 * C), f32),
            pltpu.VMEM((192, 256), f32),
            pltpu.VMEM((144, C), f32),
            pltpu.VMEM((384, C), f32),
            pltpu.VMEM((384, C), f32),
            pltpu.VMEM((2 * HALO, LON, C), bf16),
            pltpu.VMEM((2 * HALO, PAIRS, 2 * C), bf16),
            pltpu.VMEM((32, 896), f32),
            pltpu.VMEM((2, 16, 128), f32),
            pltpu.VMEM((members, 16, 128), bf16),
            pltpu.VMEM((members, 16, 128), bf16),
            pltpu.SemaphoreType.DMA,
            pltpu.SemaphoreType.DMA((ROWS,)),
            pltpu.SemaphoreType.DMA((2, 2)),
            pltpu.SemaphoreType.DMA((2, 2)),
            pltpu.SemaphoreType.DMA((members,)),
            pltpu.SemaphoreType.DMA((members,)),
        ],
        compiler_params=pltpu.CompilerParams(
            vmem_limit_bytes=56 * 2**20, collective_id=0, has_side_effects=True
        ),
    )(
        band_start, band_width, hidden_vectors, target, mix_weight, basis_coef,
        rescaling_factors, up_weight, down_weight, readout_matrix,
    )


def solution(mesh):
    in_specs = (P("ens", "space", None, None), P(None, "space", "ens")) + (P(),) * 8
    out_specs = (P("ens", "space", None, None), P(None, "space", "ens"))
    return jax.shard_map(body, mesh=mesh, in_specs=in_specs, out_specs=out_specs, check_vma=False)
```

time: 147 us -> 77.3 us (0.53)
  the two profiles are of different devices: /device:TPU:14 before, /device:TPU:1 now
where the time goes in v2:
time: 77.3 us; the launch traced here: 77 us
  Pallas kernels  69 us (89%)
  local copies, waits for them, and re-layouts  7.36 us (10%)
    pallas_call x1, Pallas kernels, body(): pl.pallas_call(step_kernel, out_shape=(jax.ShapeDtypeStruct(hidden_vector...  69 us
    unnamed x3, local copies, waits for them, and re-layouts  6.04 us

profile of v2, /device:TPU:1, one launch (start us, length us, event | category | flops | bytes accessed | tf_op | source)
XLA Modules:
  0.0 77.0 jit_solution(14523910400305016309)
XLA Ops:
  0.6 1.3 %copy.12.target = f32[2,12,45]{2,1,0:T(8,128)} copy(f32[2,12,45]{2,0,1:T(2,128)} %param.11) | data formatting | bytes 8640 | tf_op args[1]
  1.9 1.6 %copy.13.basis = bf16[2,9,4,3,192]{4,3,2,1,0:T(4,128)(2,1)} copy(bf16[2,9,4,3,192]{4,2,3,1,0:T(4,128)(2,1)} %param.13) | data formatting | bytes 165888 | tf_op args[3]
  3.5 69.0 %shard_map.113 = (bf16[1,12,720,128]{3,2,1,0:T(8,128)(2,1)}, f32[2,12,45]{2,1,0:T(8,128)}) custom-call(s32[192]{0:T(256)} %start.1, s32[192]{0:T(256)} %width.1, bf16[1,12,720,128]{3,2,1,0:T(8,128)(2,1)} %x.1, f32[2,12,45]{2,1,0:T(8,128)} %copy.12.target, bf16[2,9,128,128]{3,2,1,0:T(8,128)(2,1)} %mix.1, bf16[2,9,4,3,192]{4,3,2,1,0:T(4,128)(2,1)} %copy.13.basis, ...), custom_call_target="tpu_custom_call" | custom-call | tf_op jit(solution)/shard_map/pallas_call | solution.py:383
  72.6 1.3 %copy.14 = f32[2,12,45]{2,0,1:T(2,128)} copy(f32[2,12,45]{2,1,0:T(8,128)} %get-tuple-element.3) | data formatting | bytes 8640 | tf_op jit(solution)/shard_map/pallas_call | solution.py:383
  73.9 3.1 %copy.16 = bf16[1,12,720,128]{3,2,1,0:T(8,128)(2,1)} copy(bf16[1,12,720,128]{3,2,1,0:T(8,128)(2,1)} %get-tuple-element.6) | data formatting | bytes 4423680

commit v3 on v2

--- a/solution.py
+++ b/solution.py
@@ -49,11 +49,11 @@
     for o in range(ROWS):
         widths = jnp.where(row == o, width[me * ROWS + o], widths)
     for k in range(K):
-        for q in range(BMAX):
-            v = basis[b, k, q].astype(f32)
-            for l in range(LW):
+        for l in range(LW):
+            v = basis[b, k, l].astype(f32)
+            for q in range(BMAX):
                 at = (q * LW + l) * 16 + k
-                cf[at : at + 1, 0:192] = v[l : l + 1]
+                cf[at : at + 1, 0:192] = v[q : q + 1]
     for q in range(BMAX):
         for l in range(LW):
             at = q * LW + l
@@ -73,8 +73,8 @@
     coef = bnd[0:144, 0:16].astype(bf16)
 
     def channels(i, carry):
-        for u in range(4):
-            c = i * 4 + u
+        for u in range(8):
+            c = i * 8 + u
             rhs = jnp.concatenate(
                 [mx[pl.ds(c * 32, 16), :], mx[pl.ds(c * 32 + 16, 16), :]], axis=1
             ).astype(bf16)
@@ -83,7 +83,7 @@
             wf[pl.ds(c * 288 + 144, 144), :] = out[:, C:]
         return carry
 
-    lax.fori_loop(0, 16, channels, 0)
+    lax.fori_loop(0, 8, channels, 0)
 
     def place(o, carry):
         for q in range(BMAX):
@@ -140,7 +140,7 @@
 def step_kernel(
     start, width, x, target, mix, basis, gains, up, down, readout,
     out, score,
-    xv, ov, a, s, taps, nrm, raw, fin, mx, wf, car, cf, bnd, even, odd,
+    xv, ov, a, s, taps, nrms, fins, mx, wf, cars, cf, bnd, evens, odds,
     halo0, halo1, surf, tgt, snd, rcv,
     x_sem, out_sem, send_sem, recv_sem, ens_send, ens_recv,
 ):
@@ -226,14 +226,14 @@
     first = me * ROWS
 
     def halo_rows(b, side):
-        def fill(i, carry):
-            at = side * HALO + i
-            row = a.at[side * (ROWS + HALO) + i]
-            if b == 0:
-                prep_row(halo0.at[at], gains[0, 0:1], row, None, nrm, raw)
-            else:
-                prep_pairs(halo1.at[at], gains[1, 0:1], row, even, odd)
-            return carry
+        def fill():
+            for i in range(HALO):
+                at = side * HALO + i
+                row = a.at[side * (ROWS + HALO) + i]
+                if b == 0:
+                    prep_row(halo0.at[at], gains[0, 0:1], row, None, nrms[i], None)
+                else:
+                    prep_pairs(halo1.at[at], gains[1, 0:1], row, evens[i], odds[i])
 
         def empty():
             for i in range(HALO):
@@ -244,7 +244,7 @@
         @pl.when(has)
         def _():
             (forward(b) if side == 0 else backward(b)).wait_recv()
-            lax.fori_loop(0, HALO, fill, 0)
+            fill()
 
         @pl.when(jnp.logical_not(has))
         def _():
@@ -252,11 +252,14 @@
 
     lead = jnp.concatenate([readout[...].astype(f32), jnp.zeros((14, C), f32)], axis=0).astype(bf16)
 
-    def rows(b, low, high):
+    def rows(b, group):
         gain2 = gains[b, 1:2]
         up_matrix, down_matrix = up[b], down[b]
-
-        def row(o, carry):
+        for o, car in zip(group, cars):
+            conv_row(o, start, first, a, s, taps, car)
+        for i, (o, car) in enumerate(zip(group, cars)):
+            fin = fins[i % 2]
+
             def emit(p, n, e, d):
                 if b == 0:
                     s[o, pl.ds(p, n), 0:C] = e.astype(bf16)
@@ -265,7 +268,6 @@
                     fin[pl.ds(2 * p, n, stride=2), :] = e
                     fin[pl.ds(2 * p + 1, n, stride=2), :] = d
 
-            conv_row(o, start, first, a, s, taps, car)
             mlp_row(gain2, up_matrix, down_matrix, car, emit)
             if b == 1:
                 state = fin[0:LON, :].astype(bf16)
@@ -276,38 +278,45 @@
                 )
                 surf[pl.ds(o, 1), 0:LON] = seen[0:1]
                 surf[pl.ds(16 + o, 1), 0:LON] = seen[1:2]
+
+    def inner_rows(b):
+        def some(i, carry):
+            rows(b, [HALO + 4 * i + k for k in range(4)])
             return carry
 
-        lax.fori_loop(low, high, row, 0)
+        lax.fori_loop(0, 2, some, 0)
+
+    def outer_rows(b):
+        halo_rows(b, 0)
+        halo_rows(b, 1)
+        rows(b, [0, 1, ROWS - 2, ROWS - 1])
 
     x_copy.wait()
 
     def prep0(i, carry):
-        prep_row(xv.at[i], gains[0, 0:1], a.at[i + HALO], s.at[i], nrm, raw)
-        return carry
-
-    lax.fori_loop(0, ROWS, prep0, 0)
-    rows(0, HALO, ROWS - HALO)
-    halo_rows(0, 0)
-    rows(0, 0, HALO)
+        for k in range(2):
+            o = 2 * i + k
+            prep_row(xv.at[o], gains[0, 0:1], a.at[o + HALO], s.at[o], nrms[k], fins[k])
+        return carry
+
+    lax.fori_loop(0, ROWS // 2, prep0, 0)
+    inner_rows(0)
+    outer_rows(0)
     send_backward(1)
-    halo_rows(0, 1)
-    rows(0, ROWS - HALO, ROWS)
     send_forward(1)
 
     band_rows(1, me, basis, width, cf, bnd)
     make_taps(1, mix, mx, wf, bnd, taps)
 
     def prep1(i, carry):
-        prep_pairs(s.at[i], gains[1, 0:1], a.at[i + HALO], even, odd)
-        return carry
-
-    lax.fori_loop(0, ROWS, prep1, 0)
-    rows(1, HALO, ROWS - HALO)
-    halo_rows(1, 0)
-    rows(1, 0, HALO)
-    halo_rows(1, 1)
-    rows(1, ROWS - HALO, ROWS)
+        for k in range(2):
+            o = 2 * i + k
+            prep_pairs(s.at[o], gains[1, 0:1], a.at[o + HALO], evens[k], odds[k])
+        return carry
+
+    lax.fori_loop(0, ROWS // 2, prep1, 0)
+    inner_rows(1)
+    outer_rows(1)
 
     cols = target.shape[2]
     for e in range(members):
@@ -331,8 +340,10 @@
 
     for step in range(1, members):
         deal(step).start()
-    for v in range(2):
-        tgt[v, 0:ROWS, 0:cols] = target[v]
+    for o in range(ROWS):
+        v = target[o]
+        tgt[0, o : o + 1, 0:cols] = v[0:1]
+        tgt[1, o : o + 1, 0:cols] = v[1:2]
     for step in range(1, members):
         peer = lax.rem(ens + step, members)
         pltpu.make_async_remote_copy(
@@ -351,8 +362,10 @@
         for n in range(m):
             spread = spread + jnp.abs(field[m] - field[n])
     fair = skill - spread * (1.0 / (members * (members - 1)))
-    score[0] = fair[0:ROWS, 0:cols]
-    score[1] = pltpu.roll(fair, 64, 1)[0:ROWS, 0:cols]
+    other = pltpu.roll(fair, 64, 1)
+    for o in range(ROWS):
+        score[o, 0:1, :] = fair[o : o + 1, 0:cols]
+        score[o, 1:2, :] = other[o : o + 1, 0:cols]
 
     for step in range(1, members):
         deal(step).wait_send()
@@ -380,7 +393,9 @@
     members = lax.axis_size("ens")
     vmem = pl.BlockSpec(memory_space=pltpu.VMEM)
     smem = pl.BlockSpec(memory_space=pltpu.SMEM)
-    return pl.pallas_call(
+    target = target.transpose(1, 0, 2)
+    basis_coef = basis_coef.transpose(0, 1, 3, 2, 4)
+    state, score = pl.pallas_call(
         step_kernel,
         out_shape=(
             jax.ShapeDtypeStruct(hidden_vectors.shape, bf16),
@@ -394,16 +409,15 @@
             pltpu.VMEM((ROWS + 2 * HALO, PAIRS, 4 * C), bf16),
             pltpu.VMEM((ROWS, PAIRS, 2 * C), bf16),
             pltpu.VMEM((ROWS * BMAX, 4 * C, 2 * C), bf16),
-            pltpu.VMEM((752, C), f32),
-            pltpu.VMEM((2 * PAIRS, C), f32),
-            pltpu.VMEM((2 * PAIRS, C), f32),
+            [pltpu.VMEM((752, C), f32)] * 2,
+            [pltpu.VMEM((2 * PAIRS, C), f32)] * 2,
             pltpu.VMEM((16 * C, C), f32),
             pltpu.VMEM((144 * C, C), f32),
-            pltpu.VMEM((PAIRS, 2 * C), f32),
+            [pltpu.VMEM((PAIRS, 2 * C), f32)] * 4,
             pltpu.VMEM((192, 256), f32),
             pltpu.VMEM((144, C), f32),
-            pltpu.VMEM((384, C), f32),
-            pltpu.VMEM((384, C), f32),
+            [pltpu.VMEM((384, C), f32)] * 2,
+            [pltpu.VMEM((384, C), f32)] * 2,
             pltpu.VMEM((2 * HALO, LON, C), bf16),
             pltpu.VMEM((2 * HALO, PAIRS, 2 * C), bf16),
             pltpu.VMEM((32, 896), f32),
@@ -424,6 +438,7 @@
         band_start, band_width, hidden_vectors, target, mix_weight, basis_coef,
         rescaling_factors, up_weight, down_weight, readout_matrix,
     )
+    return state, score.transpose(1, 0, 2)
 
 
 def solution(mesh):

time: 77.3 us -> 60.2 us (0.78)
  Pallas kernels: 69 us -> 55.5 us
  local copies, waits for them, and re-layouts: 7.36 us -> 3.73 us
    pallas_call x1, Pallas kernels: 69 us -> 55.5 us  [body(): pl.pallas_call(step_kernel, out_shape=(jax.ShapeDtypeStruct(hidden_vector...]
    unnamed x3 -> x4, local copies, waits for them, and re-layouts: 6.04 us -> 3.73 us
    pallas_call x1 -> x0, local copies, waits for them, and re-layouts: 1.32 us -> none  [body(): pl.pallas_call(step_kernel, out_shape=(jax.ShapeDtypeStruct(hidden_vector...]
where the time goes in v3:
time: 60.2 us; the launch traced here: 59.9 us
  Pallas kernels  55.5 us (92%)
  local copies, waits for them, and re-layouts  3.73 us (6%)
  between operations  0.65 us (1%)
    pallas_call x1, Pallas kernels, body(): pl.pallas_call(step_kernel, out_shape=(jax.ShapeDtypeStruct(hidden_vector...  55.5 us
    unnamed x4, local copies, waits for them, and re-layouts  3.73 us

profile of v3, /device:TPU:1, one launch (start us, length us, event | category | flops | bytes accessed | tf_op | source)
XLA Modules:
  0.0 59.9 jit_solution(213756141587450072)
XLA Ops:
  0.6 55.5 %shard_map.113 = (bf16[1,12,720,128]{3,2,1,0:T(8,128)(2,1)}, f32[12,2,45]{2,1,0:T(2,128)}) custom-call(s32[192]{0:T(256)} %start.1, s32[192]{0:T(256)} %width.1, bf16[1,12,720,128]{3,2,1,0:T(8,128)(2,1)} %x.1, f32[12,2,45]{2,1,0:T(2,128)} %bitcast.4, bf16[2,9,128,128]{3,2,1,0:T(8,128)(2,1)} %mix.1, bf16[2,9,3,4,192]{4,3,2,1,0:T(4,128)(2,1)} %bitcast.3, ...), custom_call_target="tpu_custom_call" | custom-call | tf_op jit(solution)/shard_map/pallas_call | solution.py:398
  56.1 0.0 copy-start
  56.1 3.1 %copy.14 = bf16[1,12,720,128]{3,2,1,0:T(8,128)(2,1)} copy(bf16[1,12,720,128]{3,2,1,0:T(8,128)(2,1)} %get-tuple-element.8) | data formatting | bytes 4423680
  59.3 0.0 copy-done
  59.3 0.6 %copy.15 = f32[2,12,45]{2,0,1:T(2,128)} copy(f32[2,12,45]{2,0,1:T(2,128)S(1)} %bitcast.5) | data formatting | bytes 8640
Async XLA Ops:
  56.1 3.1 %copy-start = (f32[12,2,45]{2,1,0:T(2,128)S(1)}, f32[12,2,45]{2,1,0:T(2,128)}, u32[]{:S(2)}) copy-start(f32[12,2,45]{2,1,0:T(2,128)} %get-tuple-element.5) | copy-start | bytes 12964

commit v4 on v3

--- a/solution.py
+++ b/solution.py
@@ -18,6 +18,7 @@
 PARTS = ((0, 192), (192, 176))
 f32 = jnp.float32
 bf16 = jnp.bfloat16
+SPAN = 145
 MESH = pl.DeviceIdType.MESH
 
 
@@ -67,34 +68,44 @@
             bnd[at * ROWS : at * ROWS + ROWS, 0:16] = part[:ROWS]
 
 
-def make_taps(b, mix, mx, wf, bnd, taps):
+def spread_mix(b, mix, mx):
     for k in range(K):
         mx[pl.ds(k, C, stride=16), :] = mix[b, k].astype(f32)
+
+
+def channels(coef, mx, wf, low, count):
+    for u in range(count):
+        c = low + u
+        rhs = jnp.concatenate(
+            [mx[pl.ds(c * 32, 16), :], mx[pl.ds(c * 32 + 16, 16), :]], axis=1
+        ).astype(bf16)
+        out = jnp.dot(coef, rhs, preferred_element_type=f32)
+        wf[pl.ds(c * 2 * SPAN, 144), :] = out[:, :C]
+        wf[pl.ds(c * 2 * SPAN + SPAN, 144), :] = out[:, C:]
+
+
+def place(o, wf, taps):
+    for q in range(BMAX):
+        i = o * BMAX + q
+        for l in range(LW):
+            w = wf[pl.ds((q * LW + l) * ROWS + o, C, stride=SPAN), :].astype(bf16)
+            taps[i, l * C : (l + 1) * C, 0:C] = w
+            taps[i, (l + 1) * C : (l + 2) * C, C : 2 * C] = w
+
+
+def make_taps(bnd, mx, wf, taps):
     coef = bnd[0:144, 0:16].astype(bf16)
 
-    def channels(i, carry):
-        for u in range(8):
-            c = i * 8 + u
-            rhs = jnp.concatenate(
-                [mx[pl.ds(c * 32, 16), :], mx[pl.ds(c * 32 + 16, 16), :]], axis=1
-            ).astype(bf16)
-            out = jnp.dot(coef, rhs, preferred_element_type=f32)
-            wf[pl.ds(c * 288, 144), :] = out[:, :C]
-            wf[pl.ds(c * 288 + 144, 144), :] = out[:, C:]
+    def some(i, carry):
+        channels(coef, mx, wf, i * 16, 16)
         return carry
 
-    lax.fori_loop(0, 8, channels, 0)
-
-    def place(o, carry):
-        for q in range(BMAX):
-            i = o * BMAX + q
-            for l in range(LW):
-                w = wf[pl.ds((q * LW + l) * ROWS + o, C, stride=144), :].astype(bf16)
-                taps[i, l * C : (l + 1) * C, 0:C] = w
-                taps[i, (l + 1) * C : (l + 2) * C, C : 2 * C] = w
+    def put(o, carry):
+        place(o, wf, taps)
         return carry
 
-    lax.fori_loop(0, ROWS, place, 0)
+    lax.fori_loop(0, 4, some, 0)
+    lax.fori_loop(0, ROWS, put, 0)
 
 
 def prep_pairs(s, gain, a, even, odd):
@@ -138,10 +149,10 @@
 
 
 def step_kernel(
-    start, width, x, target, mix, basis, gains, up, down, readout,
-    out, score,
-    xv, ov, a, s, taps, nrms, fins, mx, wf, cars, cf, bnd, evens, odds,
-    halo0, halo1, surf, tgt, snd, rcv,
+    start, width, x, mix, basis, gains, up, down, readout,
+    out, got,
+    xv, a, s, taps_by_block, nrms, fins, mx, wf, cars, cf, bnd, evens, odds,
+    halo0, halo1, surf, snd, rcv, leads, seen,
     x_sem, out_sem, send_sem, recv_sem, ens_send, ens_recv,
 ):
     me = lax.axis_index("space")
@@ -168,8 +179,9 @@
     cf[...] = jnp.zeros_like(cf)
 
     def clear(i, carry):
-        taps[i, 3 * C : 4 * C, 0:C] = jnp.zeros((C, C), bf16)
-        taps[i, 0:C, C : 2 * C] = jnp.zeros((C, C), bf16)
+        for taps in taps_by_block:
+            taps[i, 3 * C : 4 * C, 0:C] = jnp.zeros((C, C), bf16)
+            taps[i, 0:C, C : 2 * C] = jnp.zeros((C, C), bf16)
         return carry
 
     lax.fori_loop(0, ROWS * BMAX, clear, 0)
@@ -177,7 +189,10 @@
         a[i] = jnp.zeros((PAIRS, 4 * C), bf16)
         a[ROWS + HALO + i] = jnp.zeros((PAIRS, 4 * C), bf16)
     band_rows(0, me, basis, width, cf, bnd)
-    make_taps(0, mix, mx, wf, bnd, taps)
+    spread_mix(0, mix, mx)
+    make_taps(bnd, mx, wf, taps_by_block[0])
+    band_rows(1, me, basis, width, cf, bnd)
+    spread_mix(1, mix, mx)
 
     middle = (me > 0) & (me < last)
 
@@ -250,9 +265,18 @@
         def _():
             empty()
 
-    lead = jnp.concatenate([readout[...].astype(f32), jnp.zeros((14, C), f32)], axis=0).astype(bf16)
+    turned = jnp.concatenate([readout[...].astype(f32), jnp.zeros((C - 2, C), f32)], axis=0).T
+    seen_lane = jax.lax.broadcasted_iota(jnp.int32, (C, C), 1)
+    for o in range(ROWS):
+        for side in range(2):
+            at = 32 * side + o
+            lead = jnp.where(seen_lane == at, turned[:, 0:1], 0.0)
+            lead = jnp.where(seen_lane == at + 16, turned[:, 1:2], lead)
+            leads[o, side * C : (side + 1) * C, :] = lead.astype(bf16)
+    seen[...] = jnp.zeros_like(seen)
 
     def rows(b, group):
+        taps = taps_by_block[b]
         gain2 = gains[b, 1:2]
         up_matrix, down_matrix = up[b], down[b]
         for o, car in zip(group, cars):
@@ -267,21 +291,21 @@
                 else:
                     fin[pl.ds(2 * p, n, stride=2), :] = e
                     fin[pl.ds(2 * p + 1, n, stride=2), :] = d
+                    pair = jnp.concatenate([e.astype(bf16), d.astype(bf16)], axis=1)
+                    seen[pl.ds(p, n), :] += jnp.dot(
+                        pair, leads[o], preferred_element_type=f32
+                    )
 
             mlp_row(gain2, up_matrix, down_matrix, car, emit)
             if b == 1:
-                state = fin[0:LON, :].astype(bf16)
-                ov[o] = state
-                pltpu.make_async_copy(ov.at[o], out.at[0, o], out_sem.at[o]).start()
-                seen = lax.dot_general(
-                    lead, state, (((1,), (1,)), ((), ())), preferred_element_type=f32
-                )
-                surf[pl.ds(o, 1), 0:LON] = seen[0:1]
-                surf[pl.ds(16 + o, 1), 0:LON] = seen[1:2]
+                xv[o] = fin[0:LON, :].astype(bf16)
+                pltpu.make_async_copy(xv.at[o], out.at[0, o], out_sem.at[o]).start()
 
     def inner_rows(b):
         def some(i, carry):
             rows(b, [HALO + 4 * i + k for k in range(4)])
+            if b == 0:
+                channels(bnd[0:144, 0:16].astype(bf16), mx, wf, i * 32, 32)
             return carry
 
         lax.fori_loop(0, 2, some, 0)
@@ -290,6 +314,9 @@
         halo_rows(b, 0)
         halo_rows(b, 1)
         rows(b, [0, 1, ROWS - 2, ROWS - 1])
+        if b == 0:
+            for o in range(ROWS):
+                place(o, wf, taps_by_block[1])
 
     x_copy.wait()
 
@@ -305,8 +332,6 @@
     send_backward(1)
     send_forward(1)
 
-    band_rows(1, me, basis, width, cf, bnd)
-    make_taps(1, mix, mx, wf, bnd, taps)
 
     def prep1(i, carry):
         for k in range(2):
@@ -318,7 +343,13 @@
     inner_rows(1)
     outer_rows(1)
 
-    cols = target.shape[2]
+    fin = fins[0]
+    fin[pl.ds(0, PAIRS, stride=2), :] = seen[...]
+    fin[pl.ds(1, PAIRS, stride=2), :] = pltpu.roll(seen[...], C - 32, 1)
+    for t in range(0, 640, C):
+        surf[:, t : t + C] = fin[t : t + C, :].T[0:32]
+    surf[:, 640:736] = fin[640:736, :].T[0:32]
+    cols = LON // members
     for e in range(members):
         base = e * cols // 128 * 128
         turn = (256 - (e * cols - base)) % 256
@@ -340,10 +371,6 @@
 
     for step in range(1, members):
         deal(step).start()
-    for o in range(ROWS):
-        v = target[o]
-        tgt[0, o : o + 1, 0:cols] = v[0:1]
-        tgt[1, o : o + 1, 0:cols] = v[1:2]
     for step in range(1, members):
         peer = lax.rem(ens + step, members)
         pltpu.make_async_remote_copy(
@@ -354,8 +381,53 @@
             device_id={"ens": peer},
             device_id_type=MESH,
         ).wait_recv()
+    got[...] = rcv[...]
+    for step in range(1, members):
+        deal(step).wait_send()
+    for b in range(BLOCKS):
+
+        @pl.when(me < last)
+        def _():
+            forward(b).wait_send()
+
+        @pl.when(me > 0)
+        def _():
+            backward(b).wait_send()
+
+    def finish(o, carry):
+        pltpu.make_async_copy(xv.at[o], out.at[0, o], out_sem.at[o]).wait()
+        return carry
+
+    lax.fori_loop(0, ROWS, finish, 0)
+
+
+def score_kernel(
+    state, got_far, target_far, out, score_far, held, got, target, score, tgt, in_sems, sems, small
+):
+    ins = [
+        pltpu.make_async_copy(got_far, got, small.at[0]),
+        pltpu.make_async_copy(target_far, target, small.at[1]),
+    ]
+    for copy in ins:
+        copy.start()
+    arrivals = [
+        pltpu.make_async_copy(state.at[0, o], held.at[o], in_sems.at[o]) for o in range(ROWS)
+    ]
+    copies = [pltpu.make_async_copy(held.at[o], out.at[0, o], sems.at[o]) for o in range(ROWS)]
+    for arrival in arrivals:
+        arrival.start()
+    for arrival, copy in zip(arrivals, copies):
+        arrival.wait()
+        copy.start()
+    for copy in ins:
+        copy.wait()
+    members, cols = got.shape[0], target.shape[2]
+    for o in range(ROWS):
+        v = target[o]
+        tgt[0, o : o + 1, 0:cols] = v[0:1]
+        tgt[1, o : o + 1, 0:cols] = v[1:2]
     aim = both(tgt[0], tgt[1])
-    field = [rcv[m].astype(f32) for m in range(members)]
+    field = [got[m].astype(f32) for m in range(members)]
     skill = sum(jnp.abs(f - aim) for f in field) * (1.0 / members)
     spread = jnp.zeros_like(aim)
     for m in range(members):
@@ -366,24 +438,11 @@
     for o in range(ROWS):
         score[o, 0:1, :] = fair[o : o + 1, 0:cols]
         score[o, 1:2, :] = other[o : o + 1, 0:cols]
-
-    for step in range(1, members):
-        deal(step).wait_send()
-    for b in range(BLOCKS):
-
-        @pl.when(me < last)
-        def _():
-            forward(b).wait_send()
-
-        @pl.when(me > 0)
-        def _():
-            backward(b).wait_send()
-
-    def finish(o, carry):
-        pltpu.make_async_copy(ov.at[o], out.at[0, o], out_sem.at[o]).wait()
-        return carry
-
-    lax.fori_loop(0, ROWS, finish, 0)
+    result = pltpu.make_async_copy(score, score_far, small.at[2])
+    result.start()
+    result.wait()
+    for copy in copies:
+        copy.wait()
 
 
 def body(
@@ -393,26 +452,24 @@
     members = lax.axis_size("ens")
     vmem = pl.BlockSpec(memory_space=pltpu.VMEM)
     smem = pl.BlockSpec(memory_space=pltpu.SMEM)
-    target = target.transpose(1, 0, 2)
     basis_coef = basis_coef.transpose(0, 1, 3, 2, 4)
-    state, score = pl.pallas_call(
+    state, surfaces = pl.pallas_call(
         step_kernel,
         out_shape=(
             jax.ShapeDtypeStruct(hidden_vectors.shape, bf16),
-            jax.ShapeDtypeStruct(target.shape, f32),
+            jax.ShapeDtypeStruct((members, 16, 128), bf16),
         ),
-        in_specs=[smem, smem, pl.BlockSpec(memory_space=pl.ANY)] + [vmem] * 7,
+        in_specs=[smem, smem, pl.BlockSpec(memory_space=pl.ANY)] + [vmem] * 6,
         out_specs=(pl.BlockSpec(memory_space=pl.ANY), vmem),
         scratch_shapes=[
             pltpu.VMEM((ROWS, LON, C), bf16),
-            pltpu.VMEM((ROWS, LON, C), bf16),
             pltpu.VMEM((ROWS + 2 * HALO, PAIRS, 4 * C), bf16),
             pltpu.VMEM((ROWS, PAIRS, 2 * C), bf16),
-            pltpu.VMEM((ROWS * BMAX, 4 * C, 2 * C), bf16),
+            [pltpu.VMEM((ROWS * BMAX, 4 * C, 2 * C), bf16)] * 2,
             [pltpu.VMEM((752, C), f32)] * 2,
             [pltpu.VMEM((2 * PAIRS, C), f32)] * 2,
             pltpu.VMEM((16 * C, C), f32),
-            pltpu.VMEM((144 * C, C), f32),
+            pltpu.VMEM((SPAN * C, C), f32),
             [pltpu.VMEM((PAIRS, 2 * C), f32)] * 4,
             pltpu.VMEM((192, 256), f32),
             pltpu.VMEM((144, C), f32),
@@ -421,9 +478,10 @@
             pltpu.VMEM((2 * HALO, LON, C), bf16),
             pltpu.VMEM((2 * HALO, PAIRS, 2 * C), bf16),
             pltpu.VMEM((32, 896), f32),
-            pltpu.VMEM((2, 16, 128), f32),
             pltpu.VMEM((members, 16, 128), bf16),
             pltpu.VMEM((members, 16, 128), bf16),
+            pltpu.VMEM((ROWS, 2 * C, C), bf16),
+            pltpu.VMEM((PAIRS, C), f32),
             pltpu.SemaphoreType.DMA,
             pltpu.SemaphoreType.DMA((ROWS,)),
             pltpu.SemaphoreType.DMA((2, 2)),
@@ -432,12 +490,32 @@
             pltpu.SemaphoreType.DMA((members,)),
         ],
         compiler_params=pltpu.CompilerParams(
-            vmem_limit_bytes=56 * 2**20, collective_id=0, has_side_effects=True
+            vmem_limit_bytes=60 * 2**20, collective_id=0, has_side_effects=True
         ),
     )(
-        band_start, band_width, hidden_vectors, target, mix_weight, basis_coef,
+        band_start, band_width, hidden_vectors, mix_weight, basis_coef,
         rescaling_factors, up_weight, down_weight, readout_matrix,
     )
+    target = target.transpose(1, 0, 2)
+    state, score = pl.pallas_call(
+        score_kernel,
+        out_shape=(
+            jax.ShapeDtypeStruct(state.shape, bf16),
+            jax.ShapeDtypeStruct(target.shape, f32),
+        ),
+        in_specs=[pl.BlockSpec(memory_space=pl.ANY)] * 3,
+        out_specs=[pl.BlockSpec(memory_space=pl.ANY)] * 2,
+        scratch_shapes=[
+            pltpu.VMEM((ROWS, LON, C), bf16),
+            pltpu.VMEM(surfaces.shape, bf16),
+            pltpu.VMEM(target.shape, f32),
+            pltpu.VMEM(target.shape, f32),
+            pltpu.VMEM((2, 16, 128), f32),
+            pltpu.SemaphoreType.DMA((ROWS,)),
+            pltpu.SemaphoreType.DMA((ROWS,)),
+            pltpu.SemaphoreType.DMA((3,)),
+        ],
+    )(state, surfaces, target)
     return state, score.transpose(1, 0, 2)
 
 

time: 60.2 us -> 53.7 us (0.89)
  local copies, waits for them, and re-layouts: 3.73 us -> 0 us
  Pallas kernels: 55.5 us -> 52.8 us
    pallas_call x1, Pallas kernels: 55.5 us -> 50 us  [body(): pl.pallas_call(step_kernel, out_shape=(jax.ShapeDtypeStruct(hidden_vector...]
    unnamed x4 -> x0, local copies, waits for them, and re-layouts: 3.73 us -> none
    pallas_call x0 -> x1, Pallas kernels: none -> 2.77 us  [body(): pl.pallas_call(score_kernel, out_shape=(jax.ShapeDtypeStruct(state.shape,...]
where the time goes in v4:
time: 53.7 us; the launch traced here: 53.6 us
  Pallas kernels  52.8 us (98%)
  between operations  0.82 us (2%)
    pallas_call x1, Pallas kernels, body(): pl.pallas_call(step_kernel, out_shape=(jax.ShapeDtypeStruct(hidden_vector...  50 us
    pallas_call x1, Pallas kernels, body(): pl.pallas_call(score_kernel, out_shape=(jax.ShapeDtypeStruct(state.shape,...  2.77 us

profile of v4, /device:TPU:1, one launch (start us, length us, event | category | flops | bytes accessed | tf_op | source)
XLA Modules:
  0.0 53.6 jit_solution(13840971318729904512)
XLA Ops:
  0.6 50.0 %shard_map.113 = (bf16[1,12,720,128]{3,2,1,0:T(8,128)(2,1)}, bf16[16,16,128]{2,1,0:T(8,128)(2,1)}) custom-call(s32[192]{0:T(256)} %start.1, s32[192]{0:T(256)} %width.1, bf16[1,12,720,128]{3,2,1,0:T(8,128)(2,1)} %x.1, bf16[2,9,128,128]{3,2,1,0:T(8,128)(2,1)} %mix.1, bf16[2,9,3,4,192]{4,3,2,1,0:T(4,128)(2,1)} %bitcast.3, f32[2,2,128]{2,1,0:T(2,128)} %gains.1, ...), custom_call_target="tpu_custom_call" | custom-call | tf_op jit(solution)/shard_map/pallas_call | solution.py:456
  50.7 2.8 %shard_map.114 = (bf16[1,12,720,128]{3,2,1,0:T(8,128)(2,1)}, f32[12,2,45]{2,1,0:T(2,128)}) custom-call(bf16[1,12,720,128]{3,2,1,0:T(8,128)(2,1)} %get-tuple-element.6.state, bf16[16,16,128]{2,1,0:T(8,128)(2,1)} %get-tuple-element.7.got_far, f32[12,2,45]{2,1,0:T(2,128)} %bitcast.4), custom_call_target="tpu_custom_call" | custom-call | tf_op jit(solution)/shard_map/pallas_call | solution.py:500

commit v5 on v4

--- a/solution.py
+++ b/solution.py
@@ -93,10 +93,12 @@
             taps[i, (l + 1) * C : (l + 2) * C, C : 2 * C] = w
 
 
-def make_taps(bnd, mx, wf, taps):
+def taps_beside(prepare, bnd, mx, wf, taps):
     coef = bnd[0:144, 0:16].astype(bf16)
 
     def some(i, carry):
+        for k in range(3):
+            prepare(3 * i + k, k)
         channels(coef, mx, wf, i * 16, 16)
         return carry
 
@@ -151,7 +153,7 @@
 def step_kernel(
     start, width, x, mix, basis, gains, up, down, readout,
     out, got,
-    xv, a, s, taps_by_block, nrms, fins, mx, wf, cars, cf, bnd, evens, odds,
+    xv, a, s, taps, nrms, fins, mx, wf, cars, cf, bnd, evens, odds,
     halo0, halo1, surf, snd, rcv, leads, seen,
     x_sem, out_sem, send_sem, recv_sem, ens_send, ens_recv,
 ):
@@ -179,9 +181,8 @@
     cf[...] = jnp.zeros_like(cf)
 
     def clear(i, carry):
-        for taps in taps_by_block:
-            taps[i, 3 * C : 4 * C, 0:C] = jnp.zeros((C, C), bf16)
-            taps[i, 0:C, C : 2 * C] = jnp.zeros((C, C), bf16)
+        taps[i, 3 * C : 4 * C, 0:C] = jnp.zeros((C, C), bf16)
+        taps[i, 0:C, C : 2 * C] = jnp.zeros((C, C), bf16)
         return carry
 
     lax.fori_loop(0, ROWS * BMAX, clear, 0)
@@ -190,9 +191,6 @@
         a[ROWS + HALO + i] = jnp.zeros((PAIRS, 4 * C), bf16)
     band_rows(0, me, basis, width, cf, bnd)
     spread_mix(0, mix, mx)
-    make_taps(bnd, mx, wf, taps_by_block[0])
-    band_rows(1, me, basis, width, cf, bnd)
-    spread_mix(1, mix, mx)
 
     middle = (me > 0) & (me < last)
 
@@ -276,7 +274,6 @@
     seen[...] = jnp.zeros_like(seen)
 
     def rows(b, group):
-        taps = taps_by_block[b]
         gain2 = gains[b, 1:2]
         up_matrix, down_matrix = up[b], down[b]
         for o, car in zip(group, cars):
@@ -304,8 +301,6 @@
     def inner_rows(b):
         def some(i, carry):
             rows(b, [HALO + 4 * i + k for k in range(4)])
-            if b == 0:
-                channels(bnd[0:144, 0:16].astype(bf16), mx, wf, i * 32, 32)
             return carry
 
         lax.fori_loop(0, 2, some, 0)
@@ -314,32 +309,25 @@
         halo_rows(b, 0)
         halo_rows(b, 1)
         rows(b, [0, 1, ROWS - 2, ROWS - 1])
-        if b == 0:
-            for o in range(ROWS):
-                place(o, wf, taps_by_block[1])
 
     x_copy.wait()
 
-    def prep0(i, carry):
-        for k in range(2):
-            o = 2 * i + k
-            prep_row(xv.at[o], gains[0, 0:1], a.at[o + HALO], s.at[o], nrms[k], fins[k])
-        return carry
-
-    lax.fori_loop(0, ROWS // 2, prep0, 0)
+    def prep0(o, k):
+        prep_row(xv.at[o], gains[0, 0:1], a.at[o + HALO], s.at[o], nrms[k], fins[k])
+
+    taps_beside(prep0, bnd, mx, wf, taps)
     inner_rows(0)
     outer_rows(0)
     send_backward(1)
     send_forward(1)
 
-
-    def prep1(i, carry):
-        for k in range(2):
-            o = 2 * i + k
-            prep_pairs(s.at[o], gains[1, 0:1], a.at[o + HALO], evens[k], odds[k])
-        return carry
-
-    lax.fori_loop(0, ROWS // 2, prep1, 0)
+    band_rows(1, me, basis, width, cf, bnd)
+    spread_mix(1, mix, mx)
+
+    def prep1(o, k):
+        prep_pairs(s.at[o], gains[1, 0:1], a.at[o + HALO], evens[k], odds[k])
+
+    taps_beside(prep1, bnd, mx, wf, taps)
     inner_rows(1)
     outer_rows(1)
 
@@ -465,16 +453,16 @@
             pltpu.VMEM((ROWS, LON, C), bf16),
             pltpu.VMEM((ROWS + 2 * HALO, PAIRS, 4 * C), bf16),
             pltpu.VMEM((ROWS, PAIRS, 2 * C), bf16),
-            [pltpu.VMEM((ROWS * BMAX, 4 * C, 2 * C), bf16)] * 2,
-            [pltpu.VMEM((752, C), f32)] * 2,
-            [pltpu.VMEM((2 * PAIRS, C), f32)] * 2,
+            pltpu.VMEM((ROWS * BMAX, 4 * C, 2 * C), bf16),
+            [pltpu.VMEM((752, C), f32)] * 3,
+            [pltpu.VMEM((2 * PAIRS, C), f32)] * 3,
             pltpu.VMEM((16 * C, C), f32),
             pltpu.VMEM((SPAN * C, C), f32),
             [pltpu.VMEM((PAIRS, 2 * C), f32)] * 4,
             pltpu.VMEM((192, 256), f32),
             pltpu.VMEM((144, C), f32),
-            [pltpu.VMEM((384, C), f32)] * 2,
-            [pltpu.VMEM((384, C), f32)] * 2,
+            [pltpu.VMEM((384, C), f32)] * 3,
+            [pltpu.VMEM((384, C), f32)] * 3,
             pltpu.VMEM((2 * HALO, LON, C), bf16),
             pltpu.VMEM((2 * HALO, PAIRS, 2 * C), bf16),
             pltpu.VMEM((32, 896), f32),
@@ -490,7 +478,7 @@
             pltpu.SemaphoreType.DMA((members,)),
         ],
         compiler_params=pltpu.CompilerParams(
-            vmem_limit_bytes=60 * 2**20, collective_id=0, has_side_effects=True
+            vmem_limit_bytes=56 * 2**20, collective_id=0, has_side_effects=True
         ),
     )(
         band_start, band_width, hidden_vectors, mix_weight, basis_coef,

time: 53.7 us -> 52 us (0.968)
  Pallas kernels: 52.8 us -> 50.8 us
    pallas_call x1, Pallas kernels: 50 us -> 48 us  [body(): pl.pallas_call(step_kernel, out_shape=(jax.ShapeDtypeStruct(hidden_vector...]
where the time goes in v5:
time: 52 us; the launch traced here: 51.6 us
  Pallas kernels  50.8 us (98%)
  between operations  0.8 us (2%)
    pallas_call x1, Pallas kernels, body(): pl.pallas_call(step_kernel, out_shape=(jax.ShapeDtypeStruct(hidden_vector...  48 us
    pallas_call x1, Pallas kernels, body(): pl.pallas_call(score_kernel, out_shape=(jax.ShapeDtypeStruct(state.shape,...  2.77 us

profile of v5, /device:TPU:1, one launch (start us, length us, event | category | flops | bytes accessed | tf_op | source)
XLA Modules:
  0.0 51.6 jit_solution(6915344560560900009)
XLA Ops:
  0.6 48.0 %shard_map.113 = (bf16[1,12,720,128]{3,2,1,0:T(8,128)(2,1)}, bf16[16,16,128]{2,1,0:T(8,128)(2,1)}) custom-call(s32[192]{0:T(256)} %start.1, s32[192]{0:T(256)} %width.1, bf16[1,12,720,128]{3,2,1,0:T(8,128)(2,1)} %x.1, bf16[2,9,128,128]{3,2,1,0:T(8,128)(2,1)} %mix.1, bf16[2,9,3,4,192]{4,3,2,1,0:T(4,128)(2,1)} %bitcast.3, f32[2,2,128]{2,1,0:T(2,128)} %gains.1, ...), custom_call_target="tpu_custom_call" | custom-call | tf_op jit(solution)/shard_map/pallas_call | solution.py:444
  48.7 2.8 %shard_map.114 = (bf16[1,12,720,128]{3,2,1,0:T(8,128)(2,1)}, f32[12,2,45]{2,1,0:T(2,128)}) custom-call(bf16[1,12,720,128]{3,2,1,0:T(8,128)(2,1)} %get-tuple-element.6.state, bf16[16,16,128]{2,1,0:T(8,128)(2,1)} %get-tuple-element.7.got_far, f32[12,2,45]{2,1,0:T(2,128)} %bitcast.4), custom_call_target="tpu_custom_call" | custom-call | tf_op jit(solution)/shard_map/pallas_call | solution.py:488

commit v6 on v5

--- a/solution.py
+++ b/solution.py
@@ -192,6 +192,15 @@
     band_rows(0, me, basis, width, cf, bnd)
     spread_mix(0, mix, mx)
 
+    turned = jnp.concatenate([readout[...].astype(f32), jnp.zeros((C - 2, C), f32)], axis=0).T
+    seen_lane = jax.lax.broadcasted_iota(jnp.int32, (C, C), 1)
+    for o in range(ROWS):
+        for side in range(2):
+            at = 32 * side + o
+            lead = jnp.where(seen_lane == at, turned[:, 0:1], 0.0)
+            lead = jnp.where(seen_lane == at + 16, turned[:, 1:2], lead)
+            leads[o, side * C : (side + 1) * C, :] = lead.astype(bf16)
+    seen[...] = jnp.zeros_like(seen)
     middle = (me > 0) & (me < last)
 
     @pl.when(middle)
@@ -263,15 +272,6 @@
         def _():
             empty()
 
-    turned = jnp.concatenate([readout[...].astype(f32), jnp.zeros((C - 2, C), f32)], axis=0).T
-    seen_lane = jax.lax.broadcasted_iota(jnp.int32, (C, C), 1)
-    for o in range(ROWS):
-        for side in range(2):
-            at = 32 * side + o
-            lead = jnp.where(seen_lane == at, turned[:, 0:1], 0.0)
-            lead = jnp.where(seen_lane == at + 16, turned[:, 1:2], lead)
-            leads[o, side * C : (side + 1) * C, :] = lead.astype(bf16)
-    seen[...] = jnp.zeros_like(seen)
 
     def rows(b, group):
         gain2 = gains[b, 1:2]
@@ -299,11 +299,7 @@
                 pltpu.make_async_copy(xv.at[o], out.at[0, o], out_sem.at[o]).start()
 
     def inner_rows(b):
-        def some(i, carry):
-            rows(b, [HALO + 4 * i + k for k in range(4)])
-            return carry
-
-        lax.fori_loop(0, 2, some, 0)
+        rows(b, list(range(HALO, ROWS - HALO)))
 
     def outer_rows(b):
         halo_rows(b, 0)
@@ -458,7 +454,7 @@
             [pltpu.VMEM((2 * PAIRS, C), f32)] * 3,
             pltpu.VMEM((16 * C, C), f32),
             pltpu.VMEM((SPAN * C, C), f32),
-            [pltpu.VMEM((PAIRS, 2 * C), f32)] * 4,
+            [pltpu.VMEM((PAIRS, 2 * C), f32)] * 8,
             pltpu.VMEM((192, 256), f32),
             pltpu.VMEM((144, C), f32),
             [pltpu.VMEM((384, C), f32)] * 3,

time: 52 us -> 52 us (level); the launches traced: 51.6 us -> 51.1 us
    pallas_call x1, Pallas kernels: 48 us -> 47.5 us  [body(): pl.pallas_call(step_kernel, out_shape=(jax.ShapeDtypeStruct(hidden_vector...]
where the time goes in v6:
time: 52 us; the launch traced here: 51.1 us
  Pallas kernels  50.3 us (97%)
  between operations  0.82 us (2%)
    pallas_call x1, Pallas kernels, body(): pl.pallas_call(step_kernel, out_shape=(jax.ShapeDtypeStruct(hidden_vector...  47.5 us
    pallas_call x1, Pallas kernels, body(): pl.pallas_call(score_kernel, out_shape=(jax.ShapeDtypeStruct(state.shape,...  2.77 us

profile of v6, /device:TPU:1, one launch (start us, length us, event | category | flops | bytes accessed | tf_op | source)
XLA Modules:
  0.0 51.1 jit_solution(5256664649017931408)
XLA Ops:
  0.6 47.5 %shard_map.113 = (bf16[1,12,720,128]{3,2,1,0:T(8,128)(2,1)}, bf16[16,16,128]{2,1,0:T(8,128)(2,1)}) custom-call(s32[192]{0:T(256)} %start.1, s32[192]{0:T(256)} %width.1, bf16[1,12,720,128]{3,2,1,0:T(8,128)(2,1)} %x.1, bf16[2,9,128,128]{3,2,1,0:T(8,128)(2,1)} %mix.1, bf16[2,9,3,4,192]{4,3,2,1,0:T(4,128)(2,1)} %bitcast.3, f32[2,2,128]{2,1,0:T(2,128)} %gains.1, ...), custom_call_target="tpu_custom_call" | custom-call | tf_op jit(solution)/shard_map/pallas_call | solution.py:440
  48.1 2.8 %shard_map.114 = (bf16[1,12,720,128]{3,2,1,0:T(8,128)(2,1)}, f32[12,2,45]{2,1,0:T(2,128)}) custom-call(bf16[1,12,720,128]{3,2,1,0:T(8,128)(2,1)} %get-tuple-element.6.state, bf16[16,16,128]{2,1,0:T(8,128)(2,1)} %get-tuple-element.7.got_far, f32[12,2,45]{2,1,0:T(2,128)} %bitcast.4), custom_call_target="tpu_custom_call" | custom-call | tf_op jit(solution)/shard_map/pallas_call | solution.py:484
